TPU v7x, 32 devices: a whole 2x2x4 slice. The times are simulated.
32 devices in a mesh: scene: 2 (over y), az: 8 (over z, x), rg: 2 (over core).
Axes of the slice: x: 2, y: 2, z: 4, core: 2. Of those that a mesh axis runs over, the one named last changes fastest.
Arguments:
- raw_re: float32 [64, 32768], P('rg', ('scene', 'az')), parts along dimension 1, may hold values from -6 to 6
- raw_im: float32 [64, 32768], P('rg', ('scene', 'az')), parts along dimension 1, may hold values from -6 to 6
- ref_blocks: float32 [16, 64, 64], P(('scene', 'az'), None, 'rg'), parts along dimension 0, may hold values from -3.140625 to 3.140625
- owners: int32 [4], P('scene'), parts along dimension 0, may hold values from 0 to 7, as said below
- offsets: int32 [4], P('rg'), may hold values from -8 to 8
- taps: float32 [64, 8], P('rg'), may hold values from -3 to 3
Outputs:
- image_re: float32 [64, 32768], P('rg', ('scene', 'az')), parts along dimension 1
- image_im: float32 [64, 32768], P('rg', ('scene', 'az')), parts along dimension 1
There are 2 independent parts, one for each index of `scene`. A program takes and returns all parts, laid end to end along the dimension named above; an argument that names none is the same for every part. Nothing has to cross between parts.
Inputs may be any that keep to these rules, and one draw needn't show every extreme that they name: The two sub-apertures have different owners.
All inputs are finite; a program needn't handle non-finite values.
Results may differ from a plain program's by a relative error of at most 0.00014.
Values sent between devices are 32-bit elements; how exact they have to be, the bound alone decides.
No kernel may reach another device: no remote copies, remote signals or barrier semaphores. Data moves between devices by JAX's collectives and lax.ppermute only.
A program may use at most 64 MiB of HBM per device.

v0:
```python
import functools
import math

import jax
import jax.numpy as jnp
import numpy as np
from jax import lax
from jax.experimental import pallas as pl
from jax.experimental.pallas import tpu as pltpu
from jax.sharding import PartitionSpec as P

SPLIT = 4
TAPS = 8
REACH = 8
BLOCK = 16


PRECISE = lax.Precision.HIGHEST
PHASE_GAIN = 50.0


def partner_2(value, axis, stride):
    return lax.ppermute(value, axis, [(i, i ^ 1 << stride) for i in range(lax.axis_size(axis))])


def from_root(block, axis, source):
    block = jnp.where(lax.axis_index(axis) == source, block, jnp.zeros_like(block))
    return lax.psum(block, axis)


def padded_2(value, sides, width):
    for axis, dim in sides:
        size, length = (lax.axis_size(axis), value.shape[dim])
        up = [(i, (i + 1) % size) for i in range(size - 1)]
        down = [(j, i) for i, j in up]
        last = lax.slice_in_dim(value, length - width, length, axis=dim)
        initial = lax.slice_in_dim(value, 0, width, axis=dim)
        before = lax.ppermute(last, axis, up)
        after = lax.ppermute(initial, axis, down)
        value = jnp.concatenate([before, value, after], axis=dim)
    return value


def angles(numerator, denominator, sign_value):
    return sign_value * 2.0 * math.pi * numerator.astype(jnp.float32) / denominator


def rotate(signal, cosine, sine_part):
    real_part = signal[0] * cosine - signal[1] * sine_part
    imag_part = signal[0] * sine_part + signal[1] * cosine
    return jnp.stack([real_part, imag_part])


def dft_table(length_n, sign_value):
    counter = jnp.arange(length_n, dtype=jnp.int32)
    turn_count = counter[:, None] * counter[None, :] % length_n
    angle_set = angles(turn_count, length_n, sign_value)
    return (jnp.cos(angle_set), jnp.sin(angle_set))


def complex_apply(einsum_form, cosine, sine_part, signal):
    real_part = jnp.einsum(einsum_form, cosine, signal[0], precision=PRECISE) - jnp.einsum(
        einsum_form, sine_part, signal[1], precision=PRECISE
    )
    imag_part = jnp.einsum(einsum_form, cosine, signal[1], precision=PRECISE) + jnp.einsum(
        einsum_form, sine_part, signal[0], precision=PRECISE
    )
    return jnp.stack([real_part, imag_part])


def local_dft(signal, sign_value):
    rg_cols = signal.shape[1]
    az_rows = signal.shape[2]
    inner_len = az_rows // SPLIT
    shaped = signal.reshape(2, rg_cols, SPLIT, inner_len)
    first_cos, first_sin = dft_table(SPLIT, sign_value)
    first_pass = complex_apply("aj,cjk->cak", first_cos, first_sin, shaped)
    outer_idx = jnp.arange(SPLIT, dtype=jnp.int32)
    inner_idx = jnp.arange(inner_len, dtype=jnp.int32)
    twist = angles(outer_idx[:, None] * inner_idx[None, :] % az_rows, az_rows, sign_value)
    first_pass = rotate(first_pass, jnp.cos(twist)[None, :, :], jnp.sin(twist)[None, :, :])
    second_cos, second_sin = dft_table(inner_len, sign_value)
    second_pass = complex_apply("bk,cak->cba", second_cos, second_sin, first_pass)
    return second_pass.reshape(2, rg_cols, az_rows)


def butterfly_down(signal, az_place, bit_count):
    for bit_num in reversed(range(bit_count)):
        half_span = 1 << bit_num
        partner = partner_2(signal, "az", bit_num)
        is_upper = az_place >> bit_num & 1 == 1
        angle_set = angles(az_place % half_span, 2 * half_span, -1.0)
        difference = rotate(partner - signal, jnp.cos(angle_set), jnp.sin(angle_set))
        signal = jnp.where(is_upper, difference, signal + partner)
    return signal


def butterfly_up(signal, az_place, bit_count):
    for bit_num in range(bit_count):
        half_span = 1 << bit_num
        partner = partner_2(signal, "az", bit_num)
        is_upper = az_place >> bit_num & 1 == 1
        angle_set = angles(az_place % half_span, 2 * half_span, 1.0)
        cosine = jnp.cos(angle_set)
        sine_part = jnp.sin(angle_set)
        lower_new = (signal + rotate(partner, cosine, sine_part)) * 0.5
        upper_new = (partner - rotate(signal, cosine, sine_part)) * 0.5
        signal = jnp.where(is_upper, upper_new, lower_new)
    return signal


def butterfly_shards(raw_re, raw_im, ref_blocks, owners, offsets, taps):
    rg_cols = raw_re.shape[0]
    az_rows = raw_re.shape[1]
    az_count = lax.axis_size("az")
    az_place = lax.axis_index("az")
    bit_count = az_count.bit_length() - 1
    az_total = az_rows * az_count
    rg_total = rg_cols * lax.axis_size("rg")
    own_block = ref_blocks[0]
    lower_ref = from_root(own_block, "az", owners[0])
    upper_ref = from_root(own_block, "az", owners[1])
    signal = jnp.stack([raw_re, raw_im])
    signal = butterfly_down(signal, az_place, bit_count)
    column = jnp.zeros((), jnp.int32)
    for bit_num in range(bit_count):
        column = column + ((az_place >> bit_num & 1) << bit_count - 1 - bit_num)
    row_index = jnp.arange(az_rows, dtype=jnp.int32)
    twist = angles(row_index * column % az_total, az_total, -1.0)
    signal = rotate(signal, jnp.cos(twist)[None, :], jnp.sin(twist)[None, :])
    signal = local_dft(signal, -1.0)
    frequency = column + az_count * row_index
    signed = (frequency + az_total // 2) % az_total - az_total // 2
    az_freq = signed.astype(jnp.float32) / az_total
    rg_index = lax.axis_index("rg") * rg_cols + jnp.arange(rg_cols, dtype=jnp.int32)
    rg_freq = (rg_index.astype(jnp.float32) + 0.5) / (2 * rg_total) - 0.25
    model_phase = PHASE_GAIN * jnp.sqrt((1.0 + rg_freq)[:, None] ** 2 - az_freq[None, :] ** 2)
    ref_rows = own_block.shape[0]
    coarse = frequency * ref_rows // az_total
    slot_index = jnp.where(signed >= 0, ref_rows + coarse, coarse)
    one_hot = (jnp.arange(2 * ref_rows, dtype=jnp.int32)[:, None] == slot_index[None, :]).astype(
        jnp.float32
    )
    both_refs = jnp.concatenate([lower_ref, upper_ref], axis=0)
    picked = jnp.dot(both_refs.T, one_hot, precision=PRECISE)
    phase_all = model_phase + picked
    signal = rotate(signal, jnp.cos(phase_all), jnp.sin(phase_all))
    rim_width = REACH + TAPS // 2
    padded = padded_2(signal, (("rg", 1),), rim_width)
    offset_cols = jnp.repeat(offsets, BLOCK)
    local_cols = jnp.arange(rg_cols, dtype=jnp.int32)
    tap_index = jnp.arange(TAPS, dtype=jnp.int32)
    target = local_cols[:, None] + rim_width + offset_cols[:, None] + tap_index[None, :] - TAPS // 2
    padded_index = jnp.arange(rg_cols + 2 * rim_width, dtype=jnp.int32)
    hits = (padded_index[:, None, None] == target[None, :, :]).astype(jnp.float32)
    band_matrix = jnp.sum(hits * taps[None, :, :], axis=2)
    signal = jnp.einsum("zma,mi->zia", padded, band_matrix, precision=PRECISE)
    signal = local_dft(signal, 1.0) / az_rows
    twist_back = angles(row_index * column % az_total, az_total, 1.0)
    signal = rotate(signal, jnp.cos(twist_back)[None, :], jnp.sin(twist_back)[None, :])
    signal = butterfly_up(signal, az_place, bit_count)
    return (signal[0], signal[1])


FACTOR = 128
GROUP = 4
WINDOW = 4 * GROUP
EDGE = 16


def split_bf16(value):
    high = value.astype(jnp.bfloat16)
    low = (value - high.astype(jnp.float32)).astype(jnp.bfloat16)
    return high, low


def dot_split(left, right):
    left_high, left_low = left
    right_high, right_low = right
    dot = functools.partial(jnp.dot, preferred_element_type=jnp.float32)
    return dot(left_high, right_high) + (dot(left_high, right_low) + dot(left_low, right_high))


def dft_constants():
    counter = np.arange(FACTOR)
    turns = np.outer(counter, counter)
    angle = 2 * np.pi * (turns % FACTOR) / FACTOR
    cosine, sine = np.cos(angle), np.sin(angle)
    pair = []
    for matrix in (np.block([[cosine, sine], [-sine, cosine]]), np.block([[cosine, -sine], [sine, cosine]])):
        high = matrix.astype(jnp.bfloat16)
        low = (matrix - high.astype(np.float64)).astype(jnp.bfloat16)
        pair.append((high, low))
    twist = 2 * np.pi * turns / FACTOR**2
    return pair[0], pair[1], (np.cos(twist).astype(np.float32), np.sin(twist).astype(np.float32))


def cos_sin_quarters(quarters):
    whole = jnp.floor(quarters + 0.5)
    rest = (quarters - whole) * (math.pi / 2)
    square = rest * rest
    sine = rest + rest * square * (
        -1.6666654611e-1 + square * (8.3321608736e-3 + square * (-1.9515295891e-4))
    )
    cosine = 1.0 - 0.5 * square + square * square * (
        4.166664568298827e-2 + square * (-1.388731625493765e-3 + square * 2.443315711809948e-5)
    )
    number = whole.astype(jnp.int32)
    odd = (number & 1) == 1
    turned_cos = jnp.where(odd, sine, cosine)
    turned_sin = jnp.where(odd, cosine, sine)
    cos_sign = jnp.where(((number + 1) & 2) == 2, -1.0, 1.0)
    sin_sign = jnp.where((number & 2) == 2, -1.0, 1.0)
    return turned_cos * cos_sign, turned_sin * sin_sign


def window_start(chip, side, offsets_own, offsets_other):
    block = chip * 2 * GROUP // BLOCK
    blocks = offsets_own.shape[0]
    local = lax.rem(block, blocks)
    shift = jnp.where(lax.div(block, blocks) == side, offsets_own[local], offsets_other[local])
    return chip * 2 * GROUP + shift - TAPS // 2


def group_starts(side):
    return GROUP + GROUP * side, 3 * GROUP * side


def pack_kernel(re_own, im_own, re_other, im_other, ref_own, ref_other, off_own, off_other, *refs):
    messages, (re_all, im_all, ref_all) = refs[:-3], refs[-3:]
    bins, samples = re_own.shape
    part_rows = samples // FACTOR
    place, side = lax.axis_index("az"), lax.axis_index("rg")
    own_at, other_at = EDGE + side * bins, EDGE + (1 - side) * bins
    zeros = jnp.zeros((EDGE * part_rows, FACTOR), jnp.float32)
    for all_ref, own, other in ((re_all, re_own, re_other), (im_all, im_own, im_other)):
        all_ref[: EDGE * part_rows, :] = zeros
        all_ref[(EDGE + 2 * bins) * part_rows :, :] = zeros
        for base, ref in ((own_at, own), (other_at, other)):
            for tile in range(0, bins, 8):
                for row in range(part_rows):
                    all_ref[pl.ds((base + tile) * part_rows + row, 8, stride=part_rows), :] = ref[
                        tile : tile + 8, row * FACTOR : (row + 1) * FACTOR
                    ]
    ref_rows = ref_own.shape[0]
    row = lax.broadcasted_iota(jnp.int32, (ref_rows, FACTOR), 0)
    column = lax.broadcasted_iota(jnp.int32, (ref_rows, FACTOR), 1)
    spread = (column * ref_rows // FACTOR == row).astype(jnp.float32)
    ref_all[:EDGE, :] = jnp.zeros((EDGE, FACTOR), jnp.float32)
    ref_all[EDGE + 2 * bins :, :] = jnp.zeros((EDGE, FACTOR), jnp.float32)
    for at, ref in ((own_at, ref_own), (other_at, ref_other)):
        ref_all[pl.ds(pl.multiple_of(at, 16), bins), :] = lax.dot_general(
            ref[...], spread, (((0,), (0,)), ((), ())), precision=PRECISE, preferred_element_type=jnp.float32
        )
    body = GROUP * part_rows
    for step, message in enumerate(messages):
        chip = place ^ step
        start = window_start(chip, side, off_own, off_other) + EDGE
        for group, group_at in enumerate(group_starts(side)):
            rows = pl.ds(pl.multiple_of((start + group_at) * part_rows, 8), body)
            message[group, :body, :] = re_all[rows, :]
            message[group, body : 2 * body, :] = im_all[rows, :]
            for bin_num in range(GROUP):
                message[group, 2 * body + bin_num, :] = ref_all[start + group_at + bin_num, :]
            message[group, 2 * body + GROUP :, :] = jnp.zeros((8 - GROUP, FACTOR), jnp.float32)


def phase_kernel(bins_total, off_own, off_other, out):
    place, side = lax.axis_index("az"), lax.axis_index("rg")
    start = window_start(place, side, off_own, off_other)
    shape = (FACTOR, FACTOR)
    frequency = lax.broadcasted_iota(jnp.int32, shape, 0) + FACTOR * lax.broadcasted_iota(jnp.int32, shape, 1)
    total = FACTOR * FACTOR
    signed = jnp.where(frequency >= total // 2, frequency - total, frequency)
    az_freq = signed.astype(jnp.float32) / total
    az_square = az_freq * az_freq
    for group, group_at in enumerate(group_starts(side)):
        for bin_num in range(GROUP):
            rg_index = (start + group_at + bin_num).astype(jnp.float32)
            rg_freq = (rg_index + 0.5) / (2 * bins_total) - 0.25
            base = (1.0 + rg_freq) * (1.0 + rg_freq)
            root = jnp.sqrt(base - az_square)
            cosine, sine = cos_sin_quarters(root * (PHASE_GAIN * 2 / math.pi))
            out[group, bin_num, 0] = cosine
            out[group, bin_num, 1] = sine


def spectrum_body(places, *refs):
    chunks, refs = refs[:places], refs[places:]
    owners, phase, high1, low1, high2, low2, twist_cos, twist_sin, out, lines, picks = refs
    place = lax.axis_index("az")
    samples = FACTOR * FACTOR // places
    part_rows = samples // FACTOR
    for step, chunk in enumerate(chunks):
        source = place ^ step
        for line in range(2 * GROUP):
            at = pl.multiple_of(line * FACTOR + source * part_rows, 8)
            lines[pl.ds(at, part_rows), :] = chunk[0, line * part_rows : (line + 1) * part_rows, :]
        picks[source] = chunk[0, 2 * GROUP * part_rows :, :]
    lane = lax.broadcasted_iota(jnp.int32, (2 * GROUP, FACTOR), 1)
    ref_phase = jnp.where(lane < FACTOR // 2, picks[owners[1]], picks[owners[0]])
    ref_cos, ref_sin = cos_sin_quarters(ref_phase * (2 / math.pi))
    first, second = (high1[...], low1[...]), (high2[...], low2[...])
    for pair in range(GROUP // 2):
        bins = (2 * pair, 2 * pair + 1)
        columns = []
        for bin_num in bins:
            real = lines[bin_num * FACTOR : (bin_num + 1) * FACTOR, :]
            imag = lines[(GROUP + bin_num) * FACTOR : (GROUP + bin_num + 1) * FACTOR, :]
            columns.append(jnp.concatenate([real, imag], axis=0))
        passed = dot_split(first, split_bf16(jnp.concatenate(columns, axis=1)))
        rows = []
        for at in range(2):
            real = passed[:FACTOR, at * FACTOR : (at + 1) * FACTOR]
            imag = passed[FACTOR:, at * FACTOR : (at + 1) * FACTOR]
            turned_real = real * twist_cos[...] + imag * twist_sin[...]
            turned_imag = imag * twist_cos[...] - real * twist_sin[...]
            rows.append(jnp.concatenate([turned_real, turned_imag], axis=1))
        passed = dot_split(split_bf16(jnp.concatenate(rows, axis=0)), second)
        for at, bin_num in enumerate(bins):
            real = passed[at * FACTOR : (at + 1) * FACTOR, :FACTOR]
            imag = passed[at * FACTOR : (at + 1) * FACTOR, FACTOR:]
            model_cos, model_sin = phase[0, bin_num, 0], phase[0, bin_num, 1]
            row_cos, row_sin = ref_cos[bin_num : bin_num + 1, :], ref_sin[bin_num : bin_num + 1, :]
            cosine = model_cos * row_cos - model_sin * row_sin
            sine = model_sin * row_cos + model_cos * row_sin
            out[bin_num, 0] = real * cosine - imag * sine
            out[bin_num, 1] = real * sine + imag * cosine


def image_kernel(places, *refs):
    shared, kept, received, taps_own, taps_other, high1, low1, high2, low2, twist_cos, twist_sin = refs[:11]
    messages, (band, lines) = refs[11:-2], refs[-2:]
    place, side = lax.axis_index("az"), lax.axis_index("rg")
    samples = FACTOR * FACTOR // places
    part_rows = samples // FACTOR
    bins_held = taps_own.shape[0]
    first_bin = place * 2 * GROUP + side * GROUP
    held = lax.div(first_bin, bins_held) == side
    local = lax.rem(first_bin, bins_held)
    weights = [
        [jnp.where(held, taps_own[local + j, t], taps_other[local + j, t]) for t in range(TAPS)] for j in range(GROUP)
    ]
    is_first = side == 0
    strip = 16
    for part in range(2):
        for at in range(0, FACTOR, strip):
            rows = slice(at, at + strip)
            sums = [None] * GROUP
            for slot in range(3 * GROUP):
                if slot < GROUP:
                    value = jnp.where(is_first, kept[slot, part, rows], received[slot, part, rows])
                elif slot < 2 * GROUP:
                    value = shared[slot - GROUP, part, rows]
                else:
                    at_slot = slot - 2 * GROUP
                    value = jnp.where(is_first, received[at_slot, part, rows], kept[at_slot, part, rows])
                for j in range(GROUP):
                    if 0 <= slot - j < TAPS:
                        term = value * weights[j][slot - j]
                        sums[j] = term if sums[j] is None else sums[j] + term
            for j in range(GROUP):
                band[j * FACTOR + at : j * FACTOR + at + strip, part * FACTOR : (part + 1) * FACTOR] = sums[j]
    first, second = (high1[...], low1[...]), (high2[...], low2[...])
    scale = 1.0 / (FACTOR * FACTOR)
    cos_table, sin_table = twist_cos[...] * scale, twist_sin[...] * scale
    for pair in range(GROUP // 2):
        bins = (2 * pair, 2 * pair + 1)
        passed = dot_split(split_bf16(band[2 * pair * FACTOR : (2 * pair + 2) * FACTOR, :]), first)
        columns = []
        for at in range(2):
            real = passed[at * FACTOR : (at + 1) * FACTOR, :FACTOR]
            imag = passed[at * FACTOR : (at + 1) * FACTOR, FACTOR:]
            turned_real = real * cos_table - imag * sin_table
            turned_imag = imag * cos_table + real * sin_table
            columns.append(jnp.concatenate([turned_real, turned_imag], axis=0))
        passed = dot_split(second, split_bf16(jnp.concatenate(columns, axis=1)))
        for at, bin_num in enumerate(bins):
            for part in range(2):
                lines[(part * GROUP + bin_num) * FACTOR : (part * GROUP + bin_num + 1) * FACTOR, :] = passed[
                    part * FACTOR : (part + 1) * FACTOR, at * FACTOR : (at + 1) * FACTOR
                ]
    index = lax.rem(place, places // 2) * 2 + side
    for step, message in enumerate(messages):
        chip = index ^ step
        for line in range(2 * GROUP):
            at = pl.multiple_of(line * FACTOR + chip * part_rows, 8)
            message[line * part_rows : (line + 1) * part_rows, :] = lines[pl.ds(at, part_rows), :]


def place_kernel(*refs):
    messages, (out_re, out_im, re_all, im_all) = refs[:-4], refs[-4:]
    bins, samples = out_re.shape
    part_rows = samples // FACTOR
    body = GROUP * part_rows
    place = lax.axis_index("az")
    for step, message in enumerate(messages):
        at = pl.multiple_of((place ^ step) * body, 8)
        re_all[pl.ds(at, body), :] = message[:body, :]
        im_all[pl.ds(at, body), :] = message[body:, :]
    for out, all_ref in ((out_re, re_all), (out_im, im_all)):
        for tile in range(0, bins, 8):
            for row in range(part_rows):
                out[tile : tile + 8, row * FACTOR : (row + 1) * FACTOR] = all_ref[
                    pl.ds(tile * part_rows + row, 8, stride=part_rows), :
                ]


VMEM = pl.BlockSpec(memory_space=pltpu.VMEM)
SMEM = pl.BlockSpec(memory_space=pltpu.SMEM)
KERNEL = pltpu.CompilerParams(vmem_limit_bytes=32 * 1024 * 1024)


def cost(flops, count):
    return pl.CostEstimate(flops=flops, bytes_accessed=count, transcendentals=0)


def transposed_shards(raw_re, raw_im, ref_blocks, owners, offsets, taps):
    bins, samples = raw_re.shape
    places = lax.axis_size("az")
    f32 = jnp.float32
    tables = dft_constants()
    matrices = [jnp.asarray(part) for pair in tables[:2] for part in pair]
    twists = [jnp.asarray(part) for part in tables[2]]
    ref_own = ref_blocks[0]
    swap = functools.partial(lax.ppermute, axis_name="rg", perm=[(0, 1), (1, 0)])
    offsets_other = swap(offsets)
    ref_other, re_other, im_other, taps_other = swap(ref_own), swap(raw_re), swap(raw_im), swap(taps)

    part_rows = samples // FACTOR
    message = jax.ShapeDtypeStruct((2, 2 * GROUP * part_rows + 8, FACTOR), f32)
    messages = pl.pallas_call(
        pack_kernel,
        out_shape=[message] * places,
        in_specs=[VMEM] * 6 + [SMEM] * 2,
        out_specs=[VMEM] * places,
        scratch_shapes=[
            pltpu.VMEM(((2 * bins + 2 * EDGE) * part_rows, FACTOR), f32),
            pltpu.VMEM(((2 * bins + 2 * EDGE) * part_rows, FACTOR), f32),
            pltpu.VMEM((2 * bins + 2 * EDGE, FACTOR), f32),
        ],
        compiler_params=KERNEL,
        cost_estimate=cost(10**6, 4 * 10**6),
        name="pack",
    )(raw_re, raw_im, re_other, im_other, ref_own, ref_other, offsets, offsets_other)
    chunks = [messages[0]] + [
        lax.ppermute(messages[step], "az", [(i, i ^ step) for i in range(places)]) for step in range(1, places)
    ]

    phases = pl.pallas_call(
        functools.partial(phase_kernel, 2 * bins),
        out_shape=jax.ShapeDtypeStruct((2, GROUP, 2, FACTOR, FACTOR), f32),
        in_specs=[SMEM] * 2,
        out_specs=VMEM,
        compiler_params=KERNEL,
        cost_estimate=cost(10**7, 10**6),
        name="phase",
    )(offsets, offsets_other)

    def spectrum(group):
        return pl.pallas_call(
            functools.partial(spectrum_body, places),
            out_shape=jax.ShapeDtypeStruct((GROUP, 2, FACTOR, FACTOR), f32),
            grid=(1,),
            in_specs=[pl.BlockSpec((1,) + message.shape[1:], lambda i: (group, 0, 0))] * places
            + [SMEM, pl.BlockSpec((1, GROUP, 2, FACTOR, FACTOR), lambda i: (group, 0, 0, 0, 0))]
            + [VMEM] * 6,
            out_specs=VMEM,
            scratch_shapes=[
                pltpu.VMEM((2 * GROUP * FACTOR, FACTOR), f32),
                pltpu.VMEM((places, 2 * GROUP, FACTOR), f32),
            ],
            compiler_params=KERNEL,
            cost_estimate=cost(4 * 10**8, 2 * 10**6),
            name="spectrum",
        )(*chunks, owners, phases, *matrices, *twists)

    shared = spectrum(0)
    received = swap(shared)
    kept = spectrum(1)

    pieces = pl.pallas_call(
        functools.partial(image_kernel, places),
        out_shape=[jax.ShapeDtypeStruct((2 * GROUP * part_rows, FACTOR), f32)] * places,
        in_specs=[VMEM] * 3 + [SMEM] * 2 + [VMEM] * 6,
        out_specs=[VMEM] * places,
        scratch_shapes=[
            pltpu.VMEM((GROUP * FACTOR, 2 * FACTOR), f32),
            pltpu.VMEM((2 * GROUP * FACTOR, FACTOR), f32),
        ],
        compiler_params=KERNEL,
        cost_estimate=cost(4 * 10**8, 2 * 10**6),
        name="image",
    )(shared, kept, received, taps, taps_other, *matrices, *twists)

    half = places // 2
    routes = []
    for step in range(places):
        routes.append(
            [
                (p * 2 + core, (((p % half) * 2 + core) ^ step) * 2 + p // half)
                for p in range(places)
                for core in range(2)
            ]
        )
    pieces = [lax.ppermute(piece, ("az", "rg"), route) for piece, route in zip(pieces, routes)]
    return pl.pallas_call(
        place_kernel,
        out_shape=[jax.ShapeDtypeStruct((bins, samples), f32)] * 2,
        in_specs=[VMEM] * places,
        out_specs=[VMEM] * 2,
        scratch_shapes=[pltpu.VMEM((bins * part_rows, FACTOR), f32)] * 2,
        compiler_params=KERNEL,
        cost_estimate=cost(0, 10**6),
        name="place",
    )(*pieces)


def solution(mesh):
    sizes = mesh.shape

    def whole(raw_re, raw_im, ref_blocks, owners, offsets, taps):
        line = raw_re.shape[1] // sizes["scene"]
        fits = (
            sizes["rg"] == 2
            and raw_re.shape[0] == 2 * GROUP * sizes["az"]
            and line == FACTOR * FACTOR
            and line // sizes["az"] % (8 * FACTOR) == 0
            and ref_blocks.shape[1] <= FACTOR
            and FACTOR % ref_blocks.shape[1] == 0
        )
        return jax.shard_map(
            transposed_shards if fits else butterfly_shards,
            mesh=mesh,
            in_specs=(
                P("rg", ("scene", "az")),
                P("rg", ("scene", "az")),
                P(("scene", "az"), None, "rg"),
                P("scene"),
                P("rg"),
                P("rg", None),
            ),
            out_specs=(P("rg", ("scene", "az")), P("rg", ("scene", "az"))),
            check_vma=False,
        )(raw_re, raw_im, ref_blocks, owners, offsets, taps)

    return whole
```

profile of v0, /device:TPU:0, one launch (start us, length us, event | category | flops | bytes accessed | tf_op | source)
XLA Modules:
  0.0 70.9 jit_solution(708165302206381010)
XLA Ops:
  0.6 0.5 collective-permute-start
  1.2 0.8 %copy.14 = f32[1,64,32]{2,1,0:T(8,128)S(1)} copy(f32[1,64,32]{1,2,0:T(8,128)} %param.14) | data formatting | bytes 16384 | tf_op args[2]
  2.0 0.5 collective-permute-start.2
  2.5 0.2 copy-done.8
  2.7 0.4 collective-permute-start.3
  3.1 0.8 %collective-permute-done.3.off_other = s32[2]{0:T(128)S(1)} collective-permute-done((s32[2]{0:T(128)S(1)}, s32[2]{0:T(128)S(1)}, u32[]{:S(2)}, u32[]{:S(2)}) %collective-permute-start.3) | collective-permute-done | bytes 40 | tf_op jit(solution)/shard_map/ppermute | solution.py:427
  4.0 0.9 %copy-done.6 = f32[32,2048]{1,0:T(8,128)S(1)} copy-done((f32[32,2048]{1,0:T(8,128)S(1)}, f32[32,2048]{1,0:T(8,128)}, u32[]{:S(2)}) %copy-start.6) | copy-done | bytes 262168
  4.9 0.9 %copy-done.7 = f32[32,2048]{1,0:T(8,128)S(1)} copy-done((f32[32,2048]{1,0:T(8,128)S(1)}, f32[32,2048]{1,0:T(8,128)}, u32[]{:S(2)}) %copy-start.7) | copy-done | bytes 262168
  5.9 1.0 %pack.1 = (f32[2,136,128]{2,1,0:T(8,128)S(1)}, f32[2,136,128]{2,1,0:T(8,128)S(1)}, f32[2,136,128]{2,1,0:T(8,128)S(1)}, f32[2,136,128]{2,1,0:T(8,128)S(1)}, f32[2...) custom-call(f32[32,2048]{1,0:T(8,128)S(1)} %copy-done.6, ...), custom_call_target="tpu_custom_call" | custom-call | flops 1000000 | bytes 4000000 | tf_op jit(solution)/shard_map/pack/pallas_call | solution.py:432
  6.8 2.9 %collective-permute-start.4 = (f32[2,136,128]{2,1,0:T(8,128)S(1)}, f32[2,136,128]{2,1,0:T(8,128)S(1)}, u32[]{:S(2)}, u32[]{:S(2)}) collective-permute-start(f32[2,136,128]{2,1,0:T(8,128)S(1)} %get-tuple-element.19), channel_id=1, source_target_pairs={{0,2},{2,0},{4,6},{6,4},{8,10},{10,8},{12,14},{14,12},{1,3},{3,1},... | collective-permute-start | bytes 417800 | tf_op jit(solution)/shard_map/ppermute | solution.py:447
  9.7 1.6 %collective-permute-start.5 = (f32[2,136,128]{2,1,0:T(8,128)S(1)}, f32[2,136,128]{2,1,0:T(8,128)S(1)}, u32[]{:S(2)}, u32[]{:S(2)}) collective-permute-start(f32[2,136,128]{2,1,0:T(8,128)S(1)} %get-tuple-element.20), channel_id=1, source_target_pairs={{0,4},{2,6},{4,0},{6,2},{8,12},{10,14},{12,8},{14,10},{1,5},{3,7},... | collective-permute-start | bytes 417800 | tf_op jit(solution)/shard_map/ppermute | solution.py:447
  11.3 3.0 %collective-permute-start.7 = (f32[2,136,128]{2,1,0:T(8,128)S(1)}, f32[2,136,128]{2,1,0:T(8,128)S(1)}, u32[]{:S(2)}, u32[]{:S(2)}) collective-permute-start(f32[2,136,128]{2,1,0:T(8,128)S(1)} %get-tuple-element.22), channel_id=1, source_target_pairs={{0,8},{2,10},{4,12},{6,14},{8,0},{10,2},{12,4},{14,6},{1,9},{3,11}... | collective-permute-start | bytes 417800 | tf_op jit(solution)/shard_map/ppermute | solution.py:447
  14.3 1.3 %collective-permute-start.8 = (f32[2,136,128]{2,1,0:T(8,128)S(1)}, f32[2,136,128]{2,1,0:T(8,128)S(1)}, u32[]{:S(2)}, u32[]{:S(2)}) collective-permute-start(f32[2,136,128]{2,1,0:T(8,128)S(1)} %get-tuple-element.23), channel_id=1, source_target_pairs={{0,10},{2,8},{4,14},{6,12},{8,2},{10,0},{12,6},{14,4},{1,11},{3,9}... | collective-permute-start | bytes 417800 | tf_op jit(solution)/shard_map/ppermute | solution.py:447
  15.5 3.6 %collective-permute-start.9 = (f32[2,136,128]{2,1,0:T(8,128)S(1)}, f32[2,136,128]{2,1,0:T(8,128)S(1)}, u32[]{:S(2)}, u32[]{:S(2)}) collective-permute-start(f32[2,136,128]{2,1,0:T(8,128)S(1)} %get-tuple-element.24), channel_id=1, source_target_pairs={{0,12},{2,14},{4,8},{6,10},{8,4},{10,6},{12,0},{14,2},{1,13},{3,15... | collective-permute-start | bytes 417800 | tf_op jit(solution)/shard_map/ppermute | solution.py:447
  19.1 1.9 %collective-permute-done.5.refs_2_ = f32[2,136,128]{2,1,0:T(8,128)S(1)} collective-permute-done((f32[2,136,128]{2,1,0:T(8,128)S(1)}, f32[2,136,128]{2,1,0:T(8,128)S(1)}, u32[]{:S(2)}, u32[]{:S(2)}) %collective-permute-start.5) | collective-permute-done | bytes 139296 | tf_op jit(solution)/shard_map/ppermute | solution.py:447
  21.1 0.9 %collective-permute-start.10 = (f32[2,136,128]{2,1,0:T(8,128)S(1)}, f32[2,136,128]{2,1,0:T(8,128)S(1)}, u32[]{:S(2)}, u32[]{:S(2)}) collective-permute-start(f32[2,136,128]{2,1,0:T(8,128)S(1)} %get-tuple-element.25), channel_id=1, source_target_pairs={{0,14},{2,12},{4,10},{6,8},{8,6},{10,4},{12,2},{14,0},{1,15},{3,13... | collective-permute-start | bytes 417800 | tf_op jit(solution)/shard_map/ppermute | solution.py:447
  22.0 1.4 %phase.1.refs_9_ = f32[2,4,2,128,128]{4,3,2,1,0:T(8,128)S(1)} custom-call(s32[2]{0:T(128)S(1)} %copy-done.8, s32[2]{0:T(128)S(1)} %collective-permute-done.3.off_other), custom_call_target="tpu_custom_call" | custom-call | flops 10000000 | bytes 1000000 | tf_op jit(solution)/shard_map/phase/pallas_call | solution.py:450
  23.4 11.2 %collective-permute-done.8.refs_5_ = f32[2,136,128]{2,1,0:T(8,128)S(1)} collective-permute-done((f32[2,136,128]{2,1,0:T(8,128)S(1)}, f32[2,136,128]{2,1,0:T(8,128)S(1)}, u32[]{:S(2)}, u32[]{:S(2)}) %collective-permute-start.8) | collective-permute-done | bytes 139296 | tf_op jit(solution)/shard_map/ppermute | solution.py:447
  34.6 1.5 %spectrum.2.refs_0_ = f32[4,2,128,128]{3,2,1,0:T(8,128)S(1)} custom-call(f32[2,136,128]{2,1,0:T(8,128)S(1)} %get-tuple-element.18.refs_0_, f32[2,136,128]{2,1,0:T(8,128)S(1)} %collective-permute-done.4.refs_1_, f32[2,136,128]{2,1,0:T(8,128)S(1)} %collective-permute-done.5.refs_2_, f32[2,136,128]{2,1,0:T(8,128)S(1)} %collective-permute-done.6.refs_3_, ...), custom_call_target="tpu_custom_call" | custom-call | flops 400000000 | bytes 2000000 | tf_op jit(solution)/shard_map/spectrum/pallas_call | solution.py:461
  36.2 0.5 collective-permute-start.12
  36.7 1.4 %spectrum.3.refs_1_ = f32[4,2,128,128]{3,2,1,0:T(8,128)S(1)} custom-call(f32[2,136,128]{2,1,0:T(8,128)S(1)} %get-tuple-element.18.refs_0_, f32[2,136,128]{2,1,0:T(8,128)S(1)} %collective-permute-done.4.refs_1_, f32[2,136,128]{2,1,0:T(8,128)S(1)} %collective-permute-done.5.refs_2_, f32[2,136,128]{2,1,0:T(8,128)S(1)} %collective-permute-done.6.refs_3_, ...), custom_call_target="tpu_custom_call" | custom-call | flops 400000000 | bytes 2000000 | tf_op jit(solution)/shard_map/spectrum/pallas_call | solution.py:461
  38.2 2.2 %image.1 = (f32[128,128]{1,0:T(8,128)S(1)}, f32[128,128]{1,0:T(8,128)S(1)}, f32[128,128]{1,0:T(8,128)S(1)}, f32[128,128]{1,0:T(8,128)S(1)}, f32[128,128]{1,0:T(8...) custom-call(f32[4,2,128,128]{3,2,1,0:T(8,128)S(1)} %spectrum.2.refs_0_, ...), custom_call_target="tpu_custom_call" | custom-call | flops 400000000 | bytes 2000000 | tf_op jit(solution)/shard_map/image/pallas_call | solution.py:482
  40.4 0.7 collective-permute-start.13
  41.1 8.2 %collective-permute-start.14 = (f32[128,128]{1,0:T(8,128)S(1)}, f32[128,128]{1,0:T(8,128)S(1)}, u32[]{:S(2)}, u32[]{:S(2)}) collective-permute-start(f32[128,128]{1,0:T(8,128)S(1)} %get-tuple-element.27), channel_id=1, source_target_pairs={{0,2},{1,0},{2,6},{3,4},{4,10},{5,8},{6,14},{7,12},{8,3},{9,1},{10... | collective-permute-start | bytes 196616 | tf_op jit(solution)/shard_map/ppermute | solution.py:506
  49.3 1.2 %collective-permute-start.15 = (f32[128,128]{1,0:T(8,128)S(1)}, f32[128,128]{1,0:T(8,128)S(1)}, u32[]{:S(2)}, u32[]{:S(2)}) collective-permute-start(f32[128,128]{1,0:T(8,128)S(1)} %get-tuple-element.28), channel_id=1, source_target_pairs={{0,4},{1,6},{2,0},{3,2},{4,12},{5,14},{6,8},{7,10},{8,5},{9,7},{10... | collective-permute-start | bytes 196616 | tf_op jit(solution)/shard_map/ppermute | solution.py:506
  50.6 3.4 %collective-permute-start.16 = (f32[128,128]{1,0:T(8,128)S(1)}, f32[128,128]{1,0:T(8,128)S(1)}, u32[]{:S(2)}, u32[]{:S(2)}) collective-permute-start(f32[128,128]{1,0:T(8,128)S(1)} %get-tuple-element.29), channel_id=1, source_target_pairs={{0,6},{1,4},{2,2},{3,0},{4,14},{5,12},{6,10},{7,8},{8,7},{9,5},{10... | collective-permute-start | bytes 196616 | tf_op jit(solution)/shard_map/ppermute | solution.py:506
  54.0 1.7 %collective-permute-start.17 = (f32[128,128]{1,0:T(8,128)S(1)}, f32[128,128]{1,0:T(8,128)S(1)}, u32[]{:S(2)}, u32[]{:S(2)}) collective-permute-start(f32[128,128]{1,0:T(8,128)S(1)} %get-tuple-element.30), channel_id=1, source_target_pairs={{0,8},{1,10},{2,12},{3,14},{4,0},{5,2},{6,4},{7,6},{8,9},{9,11},{1... | collective-permute-start | bytes 196616 | tf_op jit(solution)/shard_map/ppermute | solution.py:506
  55.7 2.2 %collective-permute-start.18 = (f32[128,128]{1,0:T(8,128)S(1)}, f32[128,128]{1,0:T(8,128)S(1)}, u32[]{:S(2)}, u32[]{:S(2)}) collective-permute-start(f32[128,128]{1,0:T(8,128)S(1)} %get-tuple-element.31), channel_id=1, source_target_pairs={{0,10},{1,8},{2,14},{3,12},{4,2},{5,0},{6,6},{7,4},{8,11},{9,9},{1... | collective-permute-start | bytes 196616 | tf_op jit(solution)/shard_map/ppermute | solution.py:506
  57.9 6.6 %collective-permute-start.19 = (f32[128,128]{1,0:T(8,128)S(1)}, f32[128,128]{1,0:T(8,128)S(1)}, u32[]{:S(2)}, u32[]{:S(2)}) collective-permute-start(f32[128,128]{1,0:T(8,128)S(1)} %get-tuple-element.32), channel_id=1, source_target_pairs={{0,12},{1,14},{2,8},{3,10},{4,4},{5,6},{6,0},{7,2},{8,13},{9,15},{... | collective-permute-start | bytes 196616 | tf_op jit(solution)/shard_map/ppermute | solution.py:506
  64.7 1.9 %collective-permute-done.19.refs_6_ = f32[128,128]{1,0:T(8,128)S(1)} collective-permute-done((f32[128,128]{1,0:T(8,128)S(1)}, f32[128,128]{1,0:T(8,128)S(1)}, u32[]{:S(2)}, u32[]{:S(2)}) %collective-permute-start.19) | collective-permute-done | bytes 65568 | tf_op jit(solution)/shard_map/ppermute | solution.py:506
  66.5 3.5 %collective-permute-done.20.refs_7_ = f32[128,128]{1,0:T(8,128)S(1)} collective-permute-done((f32[128,128]{1,0:T(8,128)S(1)}, f32[128,128]{1,0:T(8,128)S(1)}, u32[]{:S(2)}, u32[]{:S(2)}) %collective-permute-start.20) | collective-permute-done | bytes 65568 | tf_op jit(solution)/shard_map/ppermute | solution.py:506
  70.0 0.9 %place.1 = (f32[32,2048]{1,0:T(8,128)}, f32[32,2048]{1,0:T(8,128)}) custom-call(f32[128,128]{1,0:T(8,128)S(1)} %collective-permute-done.13.refs_0_, f32[128,128]{1,0:T(8,128)S(1)} %collective-permute-done.14.refs_1_, f32[128,128]{1,0:T(8,128)S(1)} %collective-permute-done.15.refs_2_, f32[128,128]{1,0:T(8,128)S(1)} %collective-permute-done.16.refs_3_, ...), custom_call_target="tpu_custom_call" | custom-call | bytes 1000000 | tf_op jit(solution)/shard_map/place/pallas_call | solution.py:507
  (40 shorter events, 0.4 us)
Async XLA Ops:
  0.6 3.3 %collective-permute-start = (f32[32,2048]{1,0:T(8,128)}, f32[32,2048]{1,0:T(8,128)S(1)}, u32[]{:S(2)}, u32[]{:S(2)}) collective-permute-start(f32[32,2048]{1,0:T(8,128)} %re_own.1), channel_id=1, source_target_pairs={{0,1},{1,0},{2,3},{3,2},{4,5},{5,4},{6,7},{7,6},{8,9},{9,8},{10,11... | collective-permute-start | bytes 786440 | tf_op jit(solution)/shard_map/ppermute | solution.py:428
  1.1 2.8 %collective-permute-start.1 = (f32[32,2048]{1,0:T(8,128)}, f32[32,2048]{1,0:T(8,128)S(1)}, u32[]{:S(2)}, u32[]{:S(2)}) collective-permute-start(f32[32,2048]{1,0:T(8,128)} %im_own.1), channel_id=1, source_target_pairs={{0,1},{1,0},{2,3},{3,2},{4,5},{5,4},{6,7},{7,6},{8,9},{9,8},{10,11... | collective-permute-start | bytes 786440 | tf_op jit(solution)/shard_map/ppermute | solution.py:428
  2.0 0.7 copy-start.8
  2.0 1.9 %collective-permute-start.2 = (f32[64,32]{1,0:T(8,128)S(1)}, f32[64,32]{1,0:T(8,128)S(1)}, u32[]{:S(2)}, u32[]{:S(2)}) collective-permute-start(f32[64,32]{1,0:T(8,128)S(1)} %bitcast.1), channel_id=1, source_target_pairs={{0,1},{1,0},{2,3},{3,2},{4,5},{5,4},{6,7},{7,6},{8,9},{9,8},{10,11... | collective-permute-start | bytes 24584 | tf_op jit(solution)/shard_map/ppermute | solution.py:428
  2.7 1.2 %collective-permute-start.3 = (s32[2]{0:T(128)S(1)}, s32[2]{0:T(128)S(1)}, u32[]{:S(2)}, u32[]{:S(2)}) collective-permute-start(s32[2]{0:T(128)S(1)} %copy-done.8), channel_id=1, source_target_pairs={{0,1},{1,0},{2,3},{3,2},{4,5},{5,4},{6,7},{7,6},{8,9},{9,8},{10,11... | collective-permute-start | bytes 32 | tf_op jit(solution)/shard_map/ppermute | solution.py:427
  3.9 1.0 %copy-start.6 = (f32[32,2048]{1,0:T(8,128)S(1)}, f32[32,2048]{1,0:T(8,128)}, u32[]{:S(2)}) copy-start(f32[32,2048]{1,0:T(8,128)} %re_own.1) | copy-start | bytes 786436
  4.9 0.9 %copy-start.7 = (f32[32,2048]{1,0:T(8,128)S(1)}, f32[32,2048]{1,0:T(8,128)}, u32[]{:S(2)}) copy-start(f32[32,2048]{1,0:T(8,128)} %im_own.1) | copy-start | bytes 786436
  6.8 8.7 %collective-permute-start.4 = (f32[2,136,128]{2,1,0:T(8,128)S(1)}, f32[2,136,128]{2,1,0:T(8,128)S(1)}, u32[]{:S(2)}, u32[]{:S(2)}) collective-permute-start(f32[2,136,128]{2,1,0:T(8,128)S(1)} %get-tuple-element.19), channel_id=1, source_target_pairs={{0,2},{2,0},{4,6},{6,4},{8,10},{10,8},{12,14},{14,12},{1,3},{3,1},... | collective-permute-start | bytes 417800 | tf_op jit(solution)/shard_map/ppermute | solution.py:447
  9.7 11.3 %collective-permute-start.5 = (f32[2,136,128]{2,1,0:T(8,128)S(1)}, f32[2,136,128]{2,1,0:T(8,128)S(1)}, u32[]{:S(2)}, u32[]{:S(2)}) collective-permute-start(f32[2,136,128]{2,1,0:T(8,128)S(1)} %get-tuple-element.20), channel_id=1, source_target_pairs={{0,4},{2,6},{4,0},{6,2},{8,12},{10,14},{12,8},{14,10},{1,5},{3,7},... | collective-permute-start | bytes 417800 | tf_op jit(solution)/shard_map/ppermute | solution.py:447
  11.3 12.1 %collective-permute-start.6 = (f32[2,136,128]{2,1,0:T(8,128)S(1)}, f32[2,136,128]{2,1,0:T(8,128)S(1)}, u32[]{:S(2)}, u32[]{:S(2)}) collective-permute-start(f32[2,136,128]{2,1,0:T(8,128)S(1)} %get-tuple-element.21), channel_id=1, source_target_pairs={{0,6},{2,4},{4,2},{6,0},{8,14},{10,12},{12,10},{14,8},{1,7},{3,5},... | collective-permute-start | bytes 417800 | tf_op jit(solution)/shard_map/ppermute | solution.py:447
  11.3 12.1 %collective-permute-start.7 = (f32[2,136,128]{2,1,0:T(8,128)S(1)}, f32[2,136,128]{2,1,0:T(8,128)S(1)}, u32[]{:S(2)}, u32[]{:S(2)}) collective-permute-start(f32[2,136,128]{2,1,0:T(8,128)S(1)} %get-tuple-element.22), channel_id=1, source_target_pairs={{0,8},{2,10},{4,12},{6,14},{8,0},{10,2},{12,4},{14,6},{1,9},{3,11}... | collective-permute-start | bytes 417800 | tf_op jit(solution)/shard_map/ppermute | solution.py:447
  14.3 20.2 %collective-permute-start.8 = (f32[2,136,128]{2,1,0:T(8,128)S(1)}, f32[2,136,128]{2,1,0:T(8,128)S(1)}, u32[]{:S(2)}, u32[]{:S(2)}) collective-permute-start(f32[2,136,128]{2,1,0:T(8,128)S(1)} %get-tuple-element.23), channel_id=1, source_target_pairs={{0,10},{2,8},{4,14},{6,12},{8,2},{10,0},{12,6},{14,4},{1,11},{3,9}... | collective-permute-start | bytes 417800 | tf_op jit(solution)/shard_map/ppermute | solution.py:447
  15.5 19.0 %collective-permute-start.9 = (f32[2,136,128]{2,1,0:T(8,128)S(1)}, f32[2,136,128]{2,1,0:T(8,128)S(1)}, u32[]{:S(2)}, u32[]{:S(2)}) collective-permute-start(f32[2,136,128]{2,1,0:T(8,128)S(1)} %get-tuple-element.24), channel_id=1, source_target_pairs={{0,12},{2,14},{4,8},{6,10},{8,4},{10,6},{12,0},{14,2},{1,13},{3,15... | collective-permute-start | bytes 417800 | tf_op jit(solution)/shard_map/ppermute | solution.py:447
  21.0 13.5 %copy-start = (bf16[256,256]{1,0:T(8,128)(2,1)S(1)}, bf16[256,256]{1,0:T(8,128)(2,1)}, u32[]{:S(2)}) copy-start(bf16[256,256]{1,0:T(8,128)(2,1)} %constant.12.clone.refs_10_.refs_5_) | copy-start | bytes 393220
  21.0 13.5 %copy-start.1 = (bf16[256,256]{1,0:T(8,128)(2,1)S(1)}, bf16[256,256]{1,0:T(8,128)(2,1)}, u32[]{:S(2)}) copy-start(bf16[256,256]{1,0:T(8,128)(2,1)} %constant.13.clone.refs_11_.refs_6_) | copy-start | bytes 393220
  21.0 13.5 %copy-start.2 = (bf16[256,256]{1,0:T(8,128)(2,1)S(1)}, bf16[256,256]{1,0:T(8,128)(2,1)}, u32[]{:S(2)}) copy-start(bf16[256,256]{1,0:T(8,128)(2,1)} %constant.14.clone.refs_12_.refs_7_) | copy-start | bytes 393220
  21.0 13.5 %copy-start.3 = (bf16[256,256]{1,0:T(8,128)(2,1)S(1)}, bf16[256,256]{1,0:T(8,128)(2,1)}, u32[]{:S(2)}) copy-start(bf16[256,256]{1,0:T(8,128)(2,1)} %constant.15.clone.refs_13_.refs_8_) | copy-start | bytes 393220
  21.0 13.5 %copy-start.4 = (f32[128,128]{1,0:T(8,128)S(1)}, f32[128,128]{1,0:T(8,128)}, u32[]{:S(2)}) copy-start(f32[128,128]{1,0:T(8,128)} %constant.16.clone.refs_14_.refs_9_) | copy-start | bytes 196612
  21.0 13.5 %copy-start.5 = (f32[128,128]{1,0:T(8,128)S(1)}, f32[128,128]{1,0:T(8,128)}, u32[]{:S(2)}) copy-start(f32[128,128]{1,0:T(8,128)} %constant.17.clone.refs_15_.refs_10_) | copy-start | bytes 196612
  21.1 13.5 %collective-permute-start.10 = (f32[2,136,128]{2,1,0:T(8,128)S(1)}, f32[2,136,128]{2,1,0:T(8,128)S(1)}, u32[]{:S(2)}, u32[]{:S(2)}) collective-permute-start(f32[2,136,128]{2,1,0:T(8,128)S(1)} %get-tuple-element.25), channel_id=1, source_target_pairs={{0,14},{2,12},{4,10},{6,8},{8,6},{10,4},{12,2},{14,0},{1,15},{3,13... | collective-permute-start | bytes 417800 | tf_op jit(solution)/shard_map/ppermute | solution.py:447
  23.3 11.3 %copy-start.9 = (s32[2]{0:T(128)S(1)}, s32[2]{0:T(128)}, u32[]{:S(2)}) copy-start(s32[2]{0:T(128)} %refs_8_.4) | copy-start | bytes 28
  34.6 1.6 %copy-start.10 = (f32[32,8]{0,1:T(8,128)S(1)}, f32[32,8]{0,1:T(8,128)}, u32[]{:S(2)}) copy-start(f32[32,8]{0,1:T(8,128)} %param.17) | copy-start | bytes 3076
  36.1 2.1 %collective-permute-start.11 = (f32[4,2,128,128]{3,2,1,0:T(8,128)S(1)}, f32[4,2,128,128]{3,2,1,0:T(8,128)}, u32[]{:S(2)}, u32[]{:S(2)}) collective-permute-start(f32[4,2,128,128]{3,2,1,0:T(8,128)S(1)} %spectrum.2.refs_0_), channel_id=1, source_target_pairs={{0,1},{1,0},{2,3},{3,2},{4,5},{5,4},{6,7},{7,6},{8,9},{9,8},{10,11... | collective-permute-start | bytes 1572872 | tf_op jit(solution)/shard_map/ppermute | solution.py:479
  36.2 1.9 %collective-permute-start.12 = (f32[32,8]{1,0:T(8,128)S(1)}, f32[32,8]{1,0:T(8,128)S(1)}, u32[]{:S(2)}, u32[]{:S(2)}) collective-permute-start(f32[32,8]{1,0:T(8,128)S(1)} %copy.16.refs_3_), channel_id=1, source_target_pairs={{0,1},{1,0},{2,3},{3,2},{4,5},{5,4},{6,7},{7,6},{8,9},{9,8},{10,11... | collective-permute-start | bytes 3080 | tf_op jit(solution)/shard_map/ppermute | solution.py:428
  40.4 15.3 %collective-permute-start.13 = (f32[128,128]{1,0:T(8,128)S(1)}, f32[128,128]{1,0:T(8,128)S(1)}, u32[]{:S(2)}, u32[]{:S(2)}) collective-permute-start(f32[128,128]{1,0:T(8,128)S(1)} %get-tuple-element.26), channel_id=1, source_target_pairs={{0,0},{1,2},{2,4},{3,6},{4,8},{5,10},{6,12},{7,14},{8,1},{9,3},{10... | collective-permute-start | bytes 196616 | tf_op jit(solution)/shard_map/ppermute | solution.py:506
  41.1 16.9 %collective-permute-start.14 = (f32[128,128]{1,0:T(8,128)S(1)}, f32[128,128]{1,0:T(8,128)S(1)}, u32[]{:S(2)}, u32[]{:S(2)}) collective-permute-start(f32[128,128]{1,0:T(8,128)S(1)} %get-tuple-element.27), channel_id=1, source_target_pairs={{0,2},{1,0},{2,6},{3,4},{4,10},{5,8},{6,14},{7,12},{8,3},{9,1},{10... | collective-permute-start | bytes 196616 | tf_op jit(solution)/shard_map/ppermute | solution.py:506
  49.3 15.2 %collective-permute-start.15 = (f32[128,128]{1,0:T(8,128)S(1)}, f32[128,128]{1,0:T(8,128)S(1)}, u32[]{:S(2)}, u32[]{:S(2)}) collective-permute-start(f32[128,128]{1,0:T(8,128)S(1)} %get-tuple-element.28), channel_id=1, source_target_pairs={{0,4},{1,6},{2,0},{3,2},{4,12},{5,14},{6,8},{7,10},{8,5},{9,7},{10... | collective-permute-start | bytes 196616 | tf_op jit(solution)/shard_map/ppermute | solution.py:506
  50.6 14.1 %collective-permute-start.16 = (f32[128,128]{1,0:T(8,128)S(1)}, f32[128,128]{1,0:T(8,128)S(1)}, u32[]{:S(2)}, u32[]{:S(2)}) collective-permute-start(f32[128,128]{1,0:T(8,128)S(1)} %get-tuple-element.29), channel_id=1, source_target_pairs={{0,6},{1,4},{2,2},{3,0},{4,14},{5,12},{6,10},{7,8},{8,7},{9,5},{10... | collective-permute-start | bytes 196616 | tf_op jit(solution)/shard_map/ppermute | solution.py:506
  54.0 10.6 %collective-permute-start.17 = (f32[128,128]{1,0:T(8,128)S(1)}, f32[128,128]{1,0:T(8,128)S(1)}, u32[]{:S(2)}, u32[]{:S(2)}) collective-permute-start(f32[128,128]{1,0:T(8,128)S(1)} %get-tuple-element.30), channel_id=1, source_target_pairs={{0,8},{1,10},{2,12},{3,14},{4,0},{5,2},{6,4},{7,6},{8,9},{9,11},{1... | collective-permute-start | bytes 196616 | tf_op jit(solution)/shard_map/ppermute | solution.py:506
  55.7 9.0 %collective-permute-start.18 = (f32[128,128]{1,0:T(8,128)S(1)}, f32[128,128]{1,0:T(8,128)S(1)}, u32[]{:S(2)}, u32[]{:S(2)}) collective-permute-start(f32[128,128]{1,0:T(8,128)S(1)} %get-tuple-element.31), channel_id=1, source_target_pairs={{0,10},{1,8},{2,14},{3,12},{4,2},{5,0},{6,6},{7,4},{8,11},{9,9},{1... | collective-permute-start | bytes 196616 | tf_op jit(solution)/shard_map/ppermute | solution.py:506
  57.9 8.6 %collective-permute-start.19 = (f32[128,128]{1,0:T(8,128)S(1)}, f32[128,128]{1,0:T(8,128)S(1)}, u32[]{:S(2)}, u32[]{:S(2)}) collective-permute-start(f32[128,128]{1,0:T(8,128)S(1)} %get-tuple-element.32), channel_id=1, source_target_pairs={{0,12},{1,14},{2,8},{3,10},{4,4},{5,6},{6,0},{7,2},{8,13},{9,15},{... | collective-permute-start | bytes 196616 | tf_op jit(solution)/shard_map/ppermute | solution.py:506
  64.6 5.5 %collective-permute-start.20 = (f32[128,128]{1,0:T(8,128)S(1)}, f32[128,128]{1,0:T(8,128)S(1)}, u32[]{:S(2)}, u32[]{:S(2)}) collective-permute-start(f32[128,128]{1,0:T(8,128)S(1)} %get-tuple-element.33), channel_id=1, source_target_pairs={{0,14},{1,12},{2,10},{3,8},{4,6},{5,4},{6,2},{7,0},{8,15},{9,13},{... | collective-permute-start | bytes 196616 | tf_op jit(solution)/shard_map/ppermute | solution.py:506
where the time goes:
time: 71.3 us; the launch traced here: 70.9 us
  starting transfers between devices  39.5 us (55%)
  waiting for transfers between devices  19.2 us (27%)
  Pallas kernels  8.36 us (12%)
  local copies, waits for them, and re-layouts  2.97 us (4%)
  between operations  0.9 us (1%)
    ppermute x8, starting transfers between devices, transposed_shards(): lax.ppermute(piece, ('az', 'rg'), route)  24.2 us
    ppermute x7, starting transfers between devices, transposed_shards(): lax.ppermute(messages[step], 'az', [(i, i ^ step) for i in range(places)])  13.2 us
    ppermute x7, waiting for transfers between devices, transposed_shards(): lax.ppermute(messages[step], 'az', [(i, i ^ step) for i in range(places)])  13 us
    ppermute x8, waiting for transfers between devices, transposed_shards(): lax.ppermute(piece, ('az', 'rg'), route)  5.36 us
    unnamed x24, local copies, waits for them, and re-layouts  2.97 us
    pallas_call x2, Pallas kernels, spectrum(): pl.pallas_call(functools.partial(spectrum_body, places), out_shape=jax.Sh...  2.91 us
    pallas_call x1, Pallas kernels, transposed_shards(): pl.pallas_call(functools.partial(image_kernel, places), out_shape=[jax.Sh...  2.18 us
  transfers between devices with their start and end apart: 21, of which 5 were waited for; matrix products, arithmetic and copies ran while one was open for 1% of the time, Pallas kernels for 4%

commit v1 on v0

--- a/solution.py
+++ b/solution.py
@@ -227,10 +227,10 @@
 
 
 def pack_kernel(re_own, im_own, re_other, im_other, ref_own, ref_other, off_own, off_other, *refs):
-    messages, (re_all, im_all, ref_all) = refs[:-3], refs[-3:]
+    messages, re_all, im_all, ref_all = refs
     bins, samples = re_own.shape
     part_rows = samples // FACTOR
-    place, side = lax.axis_index("az"), lax.axis_index("rg")
+    side = lax.axis_index("rg")
     own_at, other_at = EDGE + side * bins, EDGE + (1 - side) * bins
     zeros = jnp.zeros((EDGE * part_rows, FACTOR), jnp.float32)
     for all_ref, own, other in ((re_all, re_own, re_other), (im_all, im_own, im_other)):
@@ -253,8 +253,8 @@
             ref[...], spread, (((0,), (0,)), ((), ())), precision=PRECISE, preferred_element_type=jnp.float32
         )
     body = GROUP * part_rows
-    for step, message in enumerate(messages):
-        chip = place ^ step
+    for chip in range(messages.shape[0]):
+        message = messages.at[chip]
         start = window_start(chip, side, off_own, off_other) + EDGE
         for group, group_at in enumerate(group_starts(side)):
             rows = pl.ds(pl.multiple_of((start + group_at) * part_rows, 8), body)
@@ -286,13 +286,11 @@
 
 
 def spectrum_body(places, *refs):
-    chunks, refs = refs[:places], refs[places:]
-    owners, phase, high1, low1, high2, low2, twist_cos, twist_sin, out, lines, picks = refs
-    place = lax.axis_index("az")
+    chunks, owners, phase, high1, low1, high2, low2, twist_cos, twist_sin, out, lines, picks = refs
     samples = FACTOR * FACTOR // places
     part_rows = samples // FACTOR
-    for step, chunk in enumerate(chunks):
-        source = place ^ step
+    for source in range(places):
+        chunk = chunks.at[source]
         for line in range(2 * GROUP):
             at = pl.multiple_of(line * FACTOR + source * part_rows, 8)
             lines[pl.ds(at, part_rows), :] = chunk[0, line * part_rows : (line + 1) * part_rows, :]
@@ -330,7 +328,7 @@
 
 def image_kernel(places, *refs):
     shared, kept, received, taps_own, taps_other, high1, low1, high2, low2, twist_cos, twist_sin = refs[:11]
-    messages, (band, lines) = refs[11:-2], refs[-2:]
+    messages, band, lines = refs[11:]
     place, side = lax.axis_index("az"), lax.axis_index("rg")
     samples = FACTOR * FACTOR // places
     part_rows = samples // FACTOR
@@ -380,24 +378,24 @@
                 lines[(part * GROUP + bin_num) * FACTOR : (part * GROUP + bin_num + 1) * FACTOR, :] = passed[
                     part * FACTOR : (part + 1) * FACTOR, at * FACTOR : (at + 1) * FACTOR
                 ]
-    index = lax.rem(place, places // 2) * 2 + side
-    for step, message in enumerate(messages):
-        chip = index ^ step
+    for chip in range(places):
+        message = messages.at[chip]
         for line in range(2 * GROUP):
-            at = pl.multiple_of(line * FACTOR + chip * part_rows, 8)
+            at = line * FACTOR + chip * part_rows
             message[line * part_rows : (line + 1) * part_rows, :] = lines[pl.ds(at, part_rows), :]
 
 
-def place_kernel(*refs):
-    messages, (out_re, out_im, re_all, im_all) = refs[:-4], refs[-4:]
+def place_kernel(own, other, out_re, out_im, re_all, im_all):
     bins, samples = out_re.shape
     part_rows = samples // FACTOR
     body = GROUP * part_rows
-    place = lax.axis_index("az")
-    for step, message in enumerate(messages):
-        at = pl.multiple_of((place ^ step) * body, 8)
-        re_all[pl.ds(at, body), :] = message[:body, :]
-        im_all[pl.ds(at, body), :] = message[body:, :]
+    half = own.shape[0] // 2
+    side = lax.axis_index("rg")
+    for step in range(half):
+        for ref, core in ((own, side), (other, 1 - side)):
+            at = pl.multiple_of((2 * step + core) * body, 8)
+            re_all[pl.ds(at, body), :] = ref[side * half + step, :body, :]
+            im_all[pl.ds(at, body), :] = ref[side * half + step, body:, :]
     for out, all_ref in ((out_re, re_all), (out_im, im_all)):
         for tile in range(0, bins, 8):
             for row in range(part_rows):
@@ -431,9 +429,9 @@
     message = jax.ShapeDtypeStruct((2, 2 * GROUP * part_rows + 8, FACTOR), f32)
     messages = pl.pallas_call(
         pack_kernel,
-        out_shape=[message] * places,
+        out_shape=jax.ShapeDtypeStruct((places,) + message.shape, f32),
         in_specs=[VMEM] * 6 + [SMEM] * 2,
-        out_specs=[VMEM] * places,
+        out_specs=VMEM,
         scratch_shapes=[
             pltpu.VMEM(((2 * bins + 2 * EDGE) * part_rows, FACTOR), f32),
             pltpu.VMEM(((2 * bins + 2 * EDGE) * part_rows, FACTOR), f32),
@@ -443,9 +441,7 @@
         cost_estimate=cost(10**6, 4 * 10**6),
         name="pack",
     )(raw_re, raw_im, re_other, im_other, ref_own, ref_other, offsets, offsets_other)
-    chunks = [messages[0]] + [
-        lax.ppermute(messages[step], "az", [(i, i ^ step) for i in range(places)]) for step in range(1, places)
-    ]
+    chunks = lax.all_to_all(messages, "az", 0, 0, tiled=True)
 
     phases = pl.pallas_call(
         functools.partial(phase_kernel, 2 * bins),
@@ -462,8 +458,11 @@
             functools.partial(spectrum_body, places),
             out_shape=jax.ShapeDtypeStruct((GROUP, 2, FACTOR, FACTOR), f32),
             grid=(1,),
-            in_specs=[pl.BlockSpec((1,) + message.shape[1:], lambda i: (group, 0, 0))] * places
-            + [SMEM, pl.BlockSpec((1, GROUP, 2, FACTOR, FACTOR), lambda i: (group, 0, 0, 0, 0))]
+            in_specs=[
+                pl.BlockSpec((places, 1) + message.shape[1:], lambda i: (0, group, 0, 0)),
+                SMEM,
+                pl.BlockSpec((1, GROUP, 2, FACTOR, FACTOR), lambda i: (group, 0, 0, 0, 0)),
+            ]
             + [VMEM] * 6,
             out_specs=VMEM,
             scratch_shapes=[
@@ -473,7 +472,7 @@
             compiler_params=KERNEL,
             cost_estimate=cost(4 * 10**8, 2 * 10**6),
             name="spectrum",
-        )(*chunks, owners, phases, *matrices, *twists)
+        )(chunks, owners, phases, *matrices, *twists)
 
     shared = spectrum(0)
     received = swap(shared)
@@ -481,9 +480,9 @@
 
     pieces = pl.pallas_call(
         functools.partial(image_kernel, places),
-        out_shape=[jax.ShapeDtypeStruct((2 * GROUP * part_rows, FACTOR), f32)] * places,
+        out_shape=jax.ShapeDtypeStruct((places, 2 * GROUP * part_rows, FACTOR), f32),
         in_specs=[VMEM] * 3 + [SMEM] * 2 + [VMEM] * 6,
-        out_specs=[VMEM] * places,
+        out_specs=VMEM,
         scratch_shapes=[
             pltpu.VMEM((GROUP * FACTOR, 2 * FACTOR), f32),
             pltpu.VMEM((2 * GROUP * FACTOR, FACTOR), f32),
@@ -493,27 +492,18 @@
         name="image",
     )(shared, kept, received, taps, taps_other, *matrices, *twists)
 
-    half = places // 2
-    routes = []
-    for step in range(places):
-        routes.append(
-            [
-                (p * 2 + core, (((p % half) * 2 + core) ^ step) * 2 + p // half)
-                for p in range(places)
-                for core in range(2)
-            ]
-        )
-    pieces = [lax.ppermute(piece, ("az", "rg"), route) for piece, route in zip(pieces, routes)]
+    pieces = lax.all_to_all(pieces, "az", 0, 0, tiled=True)
+    pieces_other = swap(pieces)
     return pl.pallas_call(
         place_kernel,
         out_shape=[jax.ShapeDtypeStruct((bins, samples), f32)] * 2,
-        in_specs=[VMEM] * places,
+        in_specs=[VMEM] * 2,
         out_specs=[VMEM] * 2,
         scratch_shapes=[pltpu.VMEM((bins * part_rows, FACTOR), f32)] * 2,
         compiler_params=KERNEL,
         cost_estimate=cost(0, 10**6),
         name="place",
-    )(*pieces)
+    )(pieces, pieces_other)
 
 
 def solution(mesh):

time: 71.3 us -> 70.3 us (0.986)
  starting transfers between devices: 39.5 us -> 8.87 us
  blocking collectives: 0 us -> 18.2 us
  waiting for transfers between devices: 19.2 us -> 29.4 us
  Pallas kernels: 8.36 us -> 9.23 us
    ppermute x15 -> x1, starting transfers between devices: 37.4 us -> 0.01 us  [transposed_shards(): pieces_other = swap(pieces)]
    all_to_all x0 -> x1, waiting for transfers between devices: none -> 26.2 us  [transposed_shards(): chunks = lax.all_to_all(messages, 'az', 0, 0, tiled=True)]
    all_to_all x0 -> x1, blocking collectives: none -> 18.2 us  [transposed_shards(): pieces = lax.all_to_all(pieces, 'az', 0, 0, tiled=True)]
    ppermute x15 -> x1, waiting for transfers between devices: 18.4 us -> 1.91 us  [transposed_shards(): pieces_other = swap(pieces)]
    all_to_all x0 -> x1, starting transfers between devices: none -> 7.15 us  [transposed_shards(): chunks = lax.all_to_all(messages, 'az', 0, 0, tiled=True)]
    pallas_call x2, Pallas kernels: 3.16 us -> 4.13 us  [the longest x1 2.13 us: transposed_shards(): pl.pallas_call(functools.partial(image_kernel, places), out_shape=jax.Sha...]
    unnamed x24 -> x26, local copies, waits for them, and re-layouts: 2.97 us -> 3.47 us
  transfers between devices with their start and end apart: 21 -> 8, of which waited for: 5 -> 3; matrix products, arithmetic and copies ran while one was open for 1% -> 1% of each run, Pallas kernels for 4% -> 4%
where the time goes in v1:
time: 70.3 us; the launch traced here: 69.9 us
  waiting for transfers between devices  29.4 us (42%)
  blocking collectives  18.2 us (26%)
  Pallas kernels  9.23 us (13%)
  starting transfers between devices  8.87 us (13%)
  local copies, waits for them, and re-layouts  3.47 us (5%)
  between operations  0.78 us (1%)
    all_to_all x1, waiting for transfers between devices, transposed_shards(): chunks = lax.all_to_all(messages, 'az', 0, 0, tiled=True)  26.2 us
    all_to_all x1, blocking collectives, transposed_shards(): pieces = lax.all_to_all(pieces, 'az', 0, 0, tiled=True)  18.2 us
    all_to_all x1, starting transfers between devices, transposed_shards(): chunks = lax.all_to_all(messages, 'az', 0, 0, tiled=True)  7.15 us
    unnamed x26, local copies, waits for them, and re-layouts  3.47 us
    pallas_call x2, Pallas kernels, spectrum(): pl.pallas_call(functools.partial(spectrum_body, places), out_shape=jax.Sh...  2.81 us
    pallas_call x1, Pallas kernels, transposed_shards(): pl.pallas_call(functools.partial(image_kernel, places), out_shape=jax.Sha...  2.13 us
    pallas_call x1, Pallas kernels, transposed_shards(): pl.pallas_call(pack_kernel, out_shape=jax.ShapeDtypeStruct((places,) + me...  2.01 us
    ppermute x1, waiting for transfers between devices, transposed_shards(): pieces_other = swap(pieces)  1.91 us
  transfers between devices with their start and end apart: 8, of which 3 were waited for; matrix products, arithmetic and copies ran while one was open for 1% of the time, Pallas kernels for 4%

profile of v1, /device:TPU:0, one launch (start us, length us, event | category | flops | bytes accessed | tf_op | source)
XLA Modules:
  0.0 69.9 jit_solution(11652656043446058314)
XLA Ops:
  0.6 0.5 collective-permute-start
  1.1 0.1 collective-permute-start.1
  1.2 0.8 %copy.14 = f32[1,64,32]{2,1,0:T(8,128)S(1)} copy(f32[1,64,32]{1,2,0:T(8,128)} %param.14) | data formatting | bytes 16384 | tf_op args[2]
  2.0 0.5 collective-permute-start.2
  2.5 0.1 collective-permute-start.3
  2.6 1.2 %collective-permute-done.3.off_other = s32[2]{0:T(128)S(1)} collective-permute-done((s32[2]{0:T(128)}, s32[2]{0:T(128)S(1)}, u32[]{:S(2)}, u32[]{:S(2)}) %collective-permute-start.3) | collective-permute-done | bytes 40 | tf_op jit(solution)/shard_map/ppermute | solution.py:425
  3.8 0.0 collective-permute-done.re_other
  3.8 0.0 collective-permute-done.1.im_other
  3.8 0.0 copy-start.6
  3.8 0.9 %copy-done.6 = f32[32,2048]{1,0:T(8,128)S(1)} copy-done((f32[32,2048]{1,0:T(8,128)S(1)}, f32[32,2048]{1,0:T(8,128)}, u32[]{:S(2)}) %copy-start.6) | copy-done | bytes 262168
  4.7 0.9 %copy-done.7 = f32[32,2048]{1,0:T(8,128)S(1)} copy-done((f32[32,2048]{1,0:T(8,128)S(1)}, f32[32,2048]{1,0:T(8,128)}, u32[]{:S(2)}) %copy-start.7) | copy-done | bytes 262168
  5.7 0.7 copy-done.8
  6.3 2.0 %pack.1 = f32[8,2,136,128]{3,2,1,0:T(8,128)} custom-call(f32[32,2048]{1,0:T(8,128)S(1)} %copy-done.6, f32[32,2048]{1,0:T(8,128)S(1)} %copy-done.7, f32[32,2048]{1,0:T(8,128)S(1)} %collective-permute-done.re_other, f32[32,2048]{1,0:T(8,128)S(1)} %collective-permute-done.1.im_other, f32[64,32]{1,0:T(8,128)S(1)} %bitcast.2, ...), custom_call_target="tpu_custom_call" | custom-call | flops 1000000 | bytes 4000000 | tf_op jit(solution)/shard_map/pack/pallas_call | solution.py:430
  8.3 0.0 copy-start.3
  8.4 0.0 copy-start.4
  8.4 0.0 copy-start.5
  8.4 0.0 copy-start.10
  8.4 7.2 %all-to-all-start = ((f32[8,2,136,128]{3,2,1,0:T(8,128)}), f32[8,2,136,128]{3,2,1,0:T(8,128)S(1)}, u32[]{:S(2)}, u32[]{:S(2)}) async-start(f32[8,2,136,128]{3,2,1,0:T(8,128)} %pack.1), calls=%async_computation | async-start | bytes 2228224 | tf_op jit(solution)/shard_map/all_to_all | solution.py:444
  15.6 1.4 %phase.1.refs_2_ = f32[2,4,2,128,128]{4,3,2,1,0:T(8,128)S(1)} custom-call(s32[2]{0:T(128)S(1)} %copy-done.9, s32[2]{0:T(128)S(1)} %collective-permute-done.3.off_other), custom_call_target="tpu_custom_call" | custom-call | flops 10000000 | bytes 1000000 | tf_op jit(solution)/shard_map/phase/pallas_call | solution.py:446
  16.9 0.0 copy-start.11
  16.9 26.2 %all-to-all-done.refs_0_ = f32[8,2,136,128]{3,2,1,0:T(8,128)S(1)} async-done(((f32[8,2,136,128]{3,2,1,0:T(8,128)}), f32[8,2,136,128]{3,2,1,0:T(8,128)S(1)}, u32[]{:S(2)}, u32[]{:S(2)}) %all-to-all-start) | async-done | bytes 1114144 | tf_op jit(solution)/shard_map/all_to_all | solution.py:444
  43.2 1.4 %spectrum.2.refs_0_ = f32[4,2,128,128]{3,2,1,0:T(8,128)S(1)} custom-call(f32[8,2,136,128]{3,2,1,0:T(8,128)S(1)} %all-to-all-done.refs_0_, s32[2]{0:T(128)S(1)} %copy-done.10, f32[2,4,2,128,128]{4,3,2,1,0:T(8,128)S(1)} %phase.1.refs_2_, bf16[256,256]{1,0:T(8,128)(2,1)S(1)} %copy-done, bf16[256,256]{1,0:T(8,128)(2,1)S(1)} %copy-done.1, ...), custom_call_target="tpu_custom_call" | custom-call | flops 400000000 | bytes 2000000 | tf_op jit(solution)/shard_map/spectrum/pallas_call | solution.py:457
  44.7 0.1 collective-permute-start.4
  44.7 0.1 copy.16.refs_3_
  44.8 0.5 collective-permute-start.5
  45.3 1.4 %spectrum.3.refs_1_ = f32[4,2,128,128]{3,2,1,0:T(8,128)S(1)} custom-call(f32[8,2,136,128]{3,2,1,0:T(8,128)S(1)} %all-to-all-done.refs_0_, s32[2]{0:T(128)S(1)} %copy-done.10, f32[2,4,2,128,128]{4,3,2,1,0:T(8,128)S(1)} %phase.1.refs_2_, bf16[256,256]{1,0:T(8,128)(2,1)S(1)} %copy-done, bf16[256,256]{1,0:T(8,128)(2,1)S(1)} %copy-done.1, ...), custom_call_target="tpu_custom_call" | custom-call | flops 400000000 | bytes 2000000 | tf_op jit(solution)/shard_map/spectrum/pallas_call | solution.py:457
  46.7 0.0 collective-permute-done.5.refs_4_
  46.7 0.0 collective-permute-done.4.refs_2_
  46.8 2.1 %image.1 = f32[8,128,128]{2,1,0:T(8,128)S(1)} custom-call(f32[4,2,128,128]{3,2,1,0:T(8,128)S(1)} %spectrum.2.refs_0_, f32[4,2,128,128]{3,2,1,0:T(8,128)S(1)} %spectrum.3.refs_1_, f32[4,2,128,128]{3,2,1,0:T(8,128)} %collective-permute-done.4.refs_2_, f32[32,8]{1,0:T(8,128)S(1)} %copy.16.refs_3_, f32[32,8]{1,0:T(8,128)S(1)} %collective-permute-done.5.refs_4_, ...), custom_call_target="tpu_custom_call" | custom-call | flops 400000000 | bytes 2000000 | tf_op jit(solution)/shard_map/image/pallas_call | solution.py:481
  48.9 18.2 %all_to_all.10.own = f32[8,128,128]{2,1,0:T(8,128)S(1)} all-to-all(f32[8,128,128]{2,1,0:T(8,128)S(1)} %image.1), channel_id=1, replica_groups=mesh['scene'=2,'az'=8,'rg'=2] {'az'}, dimensions={0} | all-to-all | bytes 1048576 | tf_op jit(solution)/shard_map/all_to_all | solution.py:495
  67.1 1.9 %collective-permute-done.6.other = f32[8,128,128]{2,1,0:T(8,128)S(1)} collective-permute-done((f32[8,128,128]{2,1,0:T(8,128)S(1)}, f32[8,128,128]{2,1,0:T(8,128)S(1)}, u32[]{:S(2)}, u32[]{:S(2)}) %collective-permute-start.6) | collective-permute-done | bytes 524320 | tf_op jit(solution)/shard_map/ppermute | solution.py:496
  69.0 0.9 %place.1 = (f32[32,2048]{1,0:T(8,128)}, f32[32,2048]{1,0:T(8,128)}) custom-call(f32[8,128,128]{2,1,0:T(8,128)S(1)} %all_to_all.10.own, f32[8,128,128]{2,1,0:T(8,128)S(1)} %collective-permute-done.6.other), custom_call_target="tpu_custom_call" | custom-call | bytes 1000000 | tf_op jit(solution)/shard_map/place/pallas_call | solution.py:497
  (17 shorter events, 0.0 us)
Async XLA Ops:
  0.6 3.1 %collective-permute-start = (f32[32,2048]{1,0:T(8,128)}, f32[32,2048]{1,0:T(8,128)S(1)}, u32[]{:S(2)}, u32[]{:S(2)}) collective-permute-start(f32[32,2048]{1,0:T(8,128)} %re_own.1), channel_id=1, source_target_pairs={{0,1},{1,0},{2,3},{3,2},{4,5},{5,4},{6,7},{7,6},{8,9},{9,8},{10,11... | collective-permute-start | bytes 786440 | tf_op jit(solution)/shard_map/ppermute | solution.py:426
  1.1 2.6 %collective-permute-start.1 = (f32[32,2048]{1,0:T(8,128)}, f32[32,2048]{1,0:T(8,128)S(1)}, u32[]{:S(2)}, u32[]{:S(2)}) collective-permute-start(f32[32,2048]{1,0:T(8,128)} %im_own.1), channel_id=1, source_target_pairs={{0,1},{1,0},{2,3},{3,2},{4,5},{5,4},{6,7},{7,6},{8,9},{9,8},{10,11... | collective-permute-start | bytes 786440 | tf_op jit(solution)/shard_map/ppermute | solution.py:426
  2.0 1.7 %collective-permute-start.2 = (f32[64,32]{1,0:T(8,128)S(1)}, f32[64,32]{1,0:T(8,128)S(1)}, u32[]{:S(2)}, u32[]{:S(2)}) collective-permute-start(f32[64,32]{1,0:T(8,128)S(1)} %bitcast.1), channel_id=1, source_target_pairs={{0,1},{1,0},{2,3},{3,2},{4,5},{5,4},{6,7},{7,6},{8,9},{9,8},{10,11... | collective-permute-start | bytes 24584 | tf_op jit(solution)/shard_map/ppermute | solution.py:426
  2.5 1.3 %collective-permute-start.3 = (s32[2]{0:T(128)}, s32[2]{0:T(128)S(1)}, u32[]{:S(2)}, u32[]{:S(2)}) collective-permute-start(s32[2]{0:T(128)} %off_own.3), channel_id=1, source_target_pairs={{0,1},{1,0},{2,3},{3,2},{4,5},{5,4},{6,7},{7,6},{8,9},{9,8},{10,11... | collective-permute-start | bytes 32 | tf_op jit(solution)/shard_map/ppermute | solution.py:425
  3.8 1.0 %copy-start.6 = (f32[32,2048]{1,0:T(8,128)S(1)}, f32[32,2048]{1,0:T(8,128)}, u32[]{:S(2)}) copy-start(f32[32,2048]{1,0:T(8,128)} %re_own.1) | copy-start | bytes 786436
  4.7 0.9 %copy-start.7 = (f32[32,2048]{1,0:T(8,128)S(1)}, f32[32,2048]{1,0:T(8,128)}, u32[]{:S(2)}) copy-start(f32[32,2048]{1,0:T(8,128)} %im_own.1) | copy-start | bytes 786436
  5.7 0.7 copy-start.8
  8.3 7.2 %copy-start.9 = (s32[2]{0:T(128)S(1)}, s32[2]{0:T(128)}, u32[]{:S(2)}) copy-start(s32[2]{0:T(128)} %off_own.3) | copy-start | bytes 28
  8.3 34.9 %copy-start = (bf16[256,256]{1,0:T(8,128)(2,1)S(1)}, bf16[256,256]{1,0:T(8,128)(2,1)}, u32[]{:S(2)}) copy-start(bf16[256,256]{1,0:T(8,128)(2,1)} %constant.12.clone.refs_3_.refs_5_) | copy-start | bytes 393220
  8.3 34.9 %copy-start.1 = (bf16[256,256]{1,0:T(8,128)(2,1)S(1)}, bf16[256,256]{1,0:T(8,128)(2,1)}, u32[]{:S(2)}) copy-start(bf16[256,256]{1,0:T(8,128)(2,1)} %constant.13.clone.refs_4_.refs_6_) | copy-start | bytes 393220
  8.3 34.9 %copy-start.2 = (bf16[256,256]{1,0:T(8,128)(2,1)S(1)}, bf16[256,256]{1,0:T(8,128)(2,1)}, u32[]{:S(2)}) copy-start(bf16[256,256]{1,0:T(8,128)(2,1)} %constant.14.clone.refs_5_.refs_7_) | copy-start | bytes 393220
  8.3 34.9 %copy-start.3 = (bf16[256,256]{1,0:T(8,128)(2,1)S(1)}, bf16[256,256]{1,0:T(8,128)(2,1)}, u32[]{:S(2)}) copy-start(bf16[256,256]{1,0:T(8,128)(2,1)} %constant.15.clone.refs_6_.refs_8_) | copy-start | bytes 393220
  8.4 34.9 %copy-start.4 = (f32[128,128]{1,0:T(8,128)S(1)}, f32[128,128]{1,0:T(8,128)}, u32[]{:S(2)}) copy-start(f32[128,128]{1,0:T(8,128)} %constant.16.clone.refs_7_.refs_9_) | copy-start | bytes 196612
  8.4 34.9 %copy-start.5 = (f32[128,128]{1,0:T(8,128)S(1)}, f32[128,128]{1,0:T(8,128)}, u32[]{:S(2)}) copy-start(f32[128,128]{1,0:T(8,128)} %constant.17.clone.refs_8_.refs_10_) | copy-start | bytes 196612
  8.4 34.8 %copy-start.10 = (s32[2]{0:T(128)S(1)}, s32[2]{0:T(128)}, u32[]{:S(2)}) copy-start(s32[2]{0:T(128)} %refs_1_.3) | copy-start | bytes 28
  8.4 34.8 %all-to-all-start = ((f32[8,2,136,128]{3,2,1,0:T(8,128)}), f32[8,2,136,128]{3,2,1,0:T(8,128)S(1)}, u32[]{:S(2)}, u32[]{:S(2)}) async-start(f32[8,2,136,128]{3,2,1,0:T(8,128)} %pack.1), calls=%async_computation | async-start | bytes 2228224 | tf_op jit(solution)/shard_map/all_to_all | solution.py:444
  16.9 27.8 %copy-start.11 = (f32[32,8]{0,1:T(8,128)S(1)}, f32[32,8]{0,1:T(8,128)}, u32[]{:S(2)}) copy-start(f32[32,8]{0,1:T(8,128)} %param.17) | copy-start | bytes 3076
  44.7 2.1 %collective-permute-start.4 = (f32[4,2,128,128]{3,2,1,0:T(8,128)S(1)}, f32[4,2,128,128]{3,2,1,0:T(8,128)}, u32[]{:S(2)}, u32[]{:S(2)}) collective-permute-start(f32[4,2,128,128]{3,2,1,0:T(8,128)S(1)} %spectrum.2.refs_0_), channel_id=1, source_target_pairs={{0,1},{1,0},{2,3},{3,2},{4,5},{5,4},{6,7},{7,6},{8,9},{9,8},{10,11... | collective-permute-start | bytes 1572872 | tf_op jit(solution)/shard_map/ppermute | solution.py:478
  44.8 1.9 %collective-permute-start.5 = (f32[32,8]{1,0:T(8,128)S(1)}, f32[32,8]{1,0:T(8,128)S(1)}, u32[]{:S(2)}, u32[]{:S(2)}) collective-permute-start(f32[32,8]{1,0:T(8,128)S(1)} %copy.16.refs_3_), channel_id=1, source_target_pairs={{0,1},{1,0},{2,3},{3,2},{4,5},{5,4},{6,7},{7,6},{8,9},{9,8},{10,11... | collective-permute-start | bytes 3080 | tf_op jit(solution)/shard_map/ppermute | solution.py:426
  67.1 1.9 %collective-permute-start.6 = (f32[8,128,128]{2,1,0:T(8,128)S(1)}, f32[8,128,128]{2,1,0:T(8,128)S(1)}, u32[]{:S(2)}, u32[]{:S(2)}) collective-permute-start(f32[8,128,128]{2,1,0:T(8,128)S(1)} %all_to_all.10.own), channel_id=1, source_target_pairs={{0,1},{1,0},{2,3},{3,2},{4,5},{5,4},{6,7},{7,6},{8,9},{9,8},{10,11... | collective-permute-start | bytes 1572872 | tf_op jit(solution)/shard_map/ppermute | solution.py:496

commit v2 on v0

--- a/solution.py
+++ b/solution.py
@@ -226,22 +226,33 @@
     return GROUP + GROUP * side, 3 * GROUP * side
 
 
-def pack_kernel(re_own, im_own, re_other, im_other, ref_own, ref_other, off_own, off_other, *refs):
+def spread_lines(target, base, source):
+    bins, samples = source.shape
+    part_rows = samples // FACTOR
+    for tile in range(0, bins, 8):
+        for row in range(part_rows):
+            target[pl.ds((base + tile) * part_rows + row, 8, stride=part_rows), :] = source[
+                tile : tile + 8, row * FACTOR : (row + 1) * FACTOR
+            ]
+
+
+def spread_kernel(re_own, im_own, re_lines, im_lines):
+    spread_lines(re_lines, 0, re_own)
+    spread_lines(im_lines, 0, im_own)
+
+
+def pack_kernel(re_lines, im_lines, re_other, im_other, ref_own, ref_other, off_own, off_other, *refs):
     messages, (re_all, im_all, ref_all) = refs[:-3], refs[-3:]
-    bins, samples = re_own.shape
+    bins, samples = re_other.shape
     part_rows = samples // FACTOR
     place, side = lax.axis_index("az"), lax.axis_index("rg")
     own_at, other_at = EDGE + side * bins, EDGE + (1 - side) * bins
     zeros = jnp.zeros((EDGE * part_rows, FACTOR), jnp.float32)
-    for all_ref, own, other in ((re_all, re_own, re_other), (im_all, im_own, im_other)):
+    for all_ref, own, other in ((re_all, re_lines, re_other), (im_all, im_lines, im_other)):
         all_ref[: EDGE * part_rows, :] = zeros
         all_ref[(EDGE + 2 * bins) * part_rows :, :] = zeros
-        for base, ref in ((own_at, own), (other_at, other)):
-            for tile in range(0, bins, 8):
-                for row in range(part_rows):
-                    all_ref[pl.ds((base + tile) * part_rows + row, 8, stride=part_rows), :] = ref[
-                        tile : tile + 8, row * FACTOR : (row + 1) * FACTOR
-                    ]
+        all_ref[pl.ds(pl.multiple_of(own_at * part_rows, 8), bins * part_rows), :] = own[...]
+        spread_lines(all_ref, other_at, other)
     ref_rows = ref_own.shape[0]
     row = lax.broadcasted_iota(jnp.int32, (ref_rows, FACTOR), 0)
     column = lax.broadcasted_iota(jnp.int32, (ref_rows, FACTOR), 1)
@@ -285,18 +296,19 @@
             out[group, bin_num, 1] = sine
 
 
-def spectrum_body(places, *refs):
+def spectrum_body(steps, group, *refs):
+    places = len(steps)
     chunks, refs = refs[:places], refs[places:]
     owners, phase, high1, low1, high2, low2, twist_cos, twist_sin, out, lines, picks = refs
     place = lax.axis_index("az")
     samples = FACTOR * FACTOR // places
     part_rows = samples // FACTOR
-    for step, chunk in enumerate(chunks):
+    for step, chunk in zip(steps, chunks):
         source = place ^ step
         for line in range(2 * GROUP):
             at = pl.multiple_of(line * FACTOR + source * part_rows, 8)
-            lines[pl.ds(at, part_rows), :] = chunk[0, line * part_rows : (line + 1) * part_rows, :]
-        picks[source] = chunk[0, 2 * GROUP * part_rows :, :]
+            lines[pl.ds(at, part_rows), :] = chunk[group, line * part_rows : (line + 1) * part_rows, :]
+        picks[source] = chunk[group, 2 * GROUP * part_rows :, :]
     lane = lax.broadcasted_iota(jnp.int32, (2 * GROUP, FACTOR), 1)
     ref_phase = jnp.where(lane < FACTOR // 2, picks[owners[1]], picks[owners[0]])
     ref_cos, ref_sin = cos_sin_quarters(ref_phase * (2 / math.pi))
@@ -320,7 +332,7 @@
         for at, bin_num in enumerate(bins):
             real = passed[at * FACTOR : (at + 1) * FACTOR, :FACTOR]
             imag = passed[at * FACTOR : (at + 1) * FACTOR, FACTOR:]
-            model_cos, model_sin = phase[0, bin_num, 0], phase[0, bin_num, 1]
+            model_cos, model_sin = phase[group, bin_num, 0], phase[group, bin_num, 1]
             row_cos, row_sin = ref_cos[bin_num : bin_num + 1, :], ref_sin[bin_num : bin_num + 1, :]
             cosine = model_cos * row_cos - model_sin * row_sin
             sine = model_sin * row_cos + model_cos * row_sin
@@ -380,9 +392,8 @@
                 lines[(part * GROUP + bin_num) * FACTOR : (part * GROUP + bin_num + 1) * FACTOR, :] = passed[
                     part * FACTOR : (part + 1) * FACTOR, at * FACTOR : (at + 1) * FACTOR
                 ]
-    index = lax.rem(place, places // 2) * 2 + side
     for step, message in enumerate(messages):
-        chip = index ^ step
+        chip = place ^ step ^ (side * (places // 2))
         for line in range(2 * GROUP):
             at = pl.multiple_of(line * FACTOR + chip * part_rows, 8)
             message[line * part_rows : (line + 1) * part_rows, :] = lines[pl.ds(at, part_rows), :]
@@ -393,9 +404,12 @@
     bins, samples = out_re.shape
     part_rows = samples // FACTOR
     body = GROUP * part_rows
-    place = lax.axis_index("az")
+    half = len(messages) // 2
+    place, side = lax.axis_index("az"), lax.axis_index("rg")
     for step, message in enumerate(messages):
-        at = pl.multiple_of((place ^ step) * body, 8)
+        chip = place ^ step
+        core = (lax.div(chip, half) != side).astype(jnp.int32)
+        at = pl.multiple_of((lax.rem(chip, half) * 2 + core) * body, 8)
         re_all[pl.ds(at, body), :] = message[:body, :]
         im_all[pl.ds(at, body), :] = message[body:, :]
     for out, all_ref in ((out_re, re_all), (out_im, im_all)):
@@ -429,6 +443,15 @@
 
     part_rows = samples // FACTOR
     message = jax.ShapeDtypeStruct((2, 2 * GROUP * part_rows + 8, FACTOR), f32)
+    lines = pl.pallas_call(
+        spread_kernel,
+        out_shape=[jax.ShapeDtypeStruct((bins * part_rows, FACTOR), f32)] * 2,
+        in_specs=[VMEM] * 2,
+        out_specs=[VMEM] * 2,
+        compiler_params=KERNEL,
+        cost_estimate=cost(0, 2 * 10**6),
+        name="spread",
+    )(raw_re, raw_im)
     messages = pl.pallas_call(
         pack_kernel,
         out_shape=[message] * places,
@@ -442,9 +465,11 @@
         compiler_params=KERNEL,
         cost_estimate=cost(10**6, 4 * 10**6),
         name="pack",
-    )(raw_re, raw_im, re_other, im_other, ref_own, ref_other, offsets, offsets_other)
-    chunks = [messages[0]] + [
-        lax.ppermute(messages[step], "az", [(i, i ^ step) for i in range(places)]) for step in range(1, places)
+    )(*lines, re_other, im_other, ref_own, ref_other, offsets, offsets_other)
+    steps = (0, 1, 2, 7, 6, 5, 4, 3)
+    chunks = [
+        lax.ppermute(messages[step], "az", [(i, i ^ step) for i in range(places)]) if step else messages[step]
+        for step in steps
     ]
 
     phases = pl.pallas_call(
@@ -459,12 +484,9 @@
 
     def spectrum(group):
         return pl.pallas_call(
-            functools.partial(spectrum_body, places),
+            functools.partial(spectrum_body, steps, group),
             out_shape=jax.ShapeDtypeStruct((GROUP, 2, FACTOR, FACTOR), f32),
-            grid=(1,),
-            in_specs=[pl.BlockSpec((1,) + message.shape[1:], lambda i: (group, 0, 0))] * places
-            + [SMEM, pl.BlockSpec((1, GROUP, 2, FACTOR, FACTOR), lambda i: (group, 0, 0, 0, 0))]
-            + [VMEM] * 6,
+            in_specs=[VMEM] * places + [SMEM] + [VMEM] * 7,
             out_specs=VMEM,
             scratch_shapes=[
                 pltpu.VMEM((2 * GROUP * FACTOR, FACTOR), f32),
@@ -494,15 +516,14 @@
     )(shared, kept, received, taps, taps_other, *matrices, *twists)
 
     half = places // 2
-    routes = []
-    for step in range(places):
-        routes.append(
-            [
-                (p * 2 + core, (((p % half) * 2 + core) ^ step) * 2 + p // half)
-                for p in range(places)
-                for core in range(2)
-            ]
-        )
+    routes = [
+        [
+            (chip * 2 + core, (chip ^ step ^ (core * half)) * 2 + chip // half)
+            for chip in range(places)
+            for core in range(2)
+        ]
+        for step in range(places)
+    ]
     pieces = [lax.ppermute(piece, ("az", "rg"), route) for piece, route in zip(pieces, routes)]
     return pl.pallas_call(
         place_kernel,

time: 71.3 us -> 65.2 us (0.914)
  the two profiles are of different devices: /device:TPU:0 before, /device:TPU:1 now
where the time goes in v2:
time: 65.2 us; the launch traced here: 64.8 us
  starting transfers between devices  27.9 us (43%)
  waiting for transfers between devices  24.4 us (37%)
  Pallas kernels  8.39 us (13%)
  local copies, waits for them, and re-layouts  3.32 us (5%)
  between operations  0.86 us (1%)
    ppermute x7, waiting for transfers between devices, transposed_shards(): lax.ppermute(messages[step], 'az', [(i, i ^ step) for i in range(places)])  17.9 us
    ppermute x8, starting transfers between devices, transposed_shards(): lax.ppermute(piece, ('az', 'rg'), route)  14.5 us
    ppermute x7, starting transfers between devices, transposed_shards(): lax.ppermute(messages[step], 'az', [(i, i ^ step) for i in range(places)])  11.3 us
    ppermute x8, waiting for transfers between devices, transposed_shards(): lax.ppermute(piece, ('az', 'rg'), route)  6.35 us
    unnamed x24, local copies, waits for them, and re-layouts  3.32 us
    pallas_call x2, Pallas kernels, spectrum(): pl.pallas_call(functools.partial(spectrum_body, steps, group), out_shape=...  2.91 us
    pallas_call x1, Pallas kernels, transposed_shards(): pl.pallas_call(functools.partial(image_kernel, places), out_shape=[jax.Sh...  2.17 us
    pallas_call x1, Pallas kernels, transposed_shards(): pl.pallas_call(functools.partial(phase_kernel, 2 * bins), out_shape=jax.S...  1.38 us
  transfers between devices with their start and end apart: 21, of which 6 were waited for; matrix products, arithmetic and copies ran while one was open for 1% of the time, Pallas kernels for 5%

profile of v2, /device:TPU:1, one launch (start us, length us, event | category | flops | bytes accessed | tf_op | source)
XLA Modules:
  0.0 64.8 jit_solution(1156889187191815741)
XLA Ops:
  0.8 0.5 collective-permute-start.1
  1.2 0.8 %copy.14 = f32[1,64,32]{2,1,0:T(8,128)S(1)} copy(f32[1,64,32]{1,2,0:T(8,128)} %param.14) | data formatting | bytes 16384 | tf_op args[2]
  2.0 0.1 collective-permute-start.2
  2.2 0.5 copy-done.8
  2.7 0.9 %copy-done.6 = f32[32,2048]{1,0:T(8,128)S(1)} copy-done((f32[32,2048]{1,0:T(8,128)S(1)}, f32[32,2048]{1,0:T(8,128)}, u32[]{:S(2)}) %copy-start.6) | copy-done | bytes 262168
  3.7 0.9 %copy-done.7 = f32[32,2048]{1,0:T(8,128)S(1)} copy-done((f32[32,2048]{1,0:T(8,128)S(1)}, f32[32,2048]{1,0:T(8,128)}, u32[]{:S(2)}) %copy-start.7) | copy-done | bytes 262168
  4.6 0.1 spread.1
  4.8 0.9 %pack.1 = (f32[2,136,128]{2,1,0:T(8,128)S(1)}, f32[2,136,128]{2,1,0:T(8,128)S(1)}, f32[2,136,128]{2,1,0:T(8,128)S(1)}, f32[2,136,128]{2,1,0:T(8,128)S(1)}, f32[2...) custom-call(f32[512,128]{1,0:T(8,128)S(1)} %get-tuple-element.20.re_, ...), custom_call_target="tpu_custom_call" | custom-call | flops 1000000 | bytes 4000000 | tf_op jit(solution)/shard_map/pack/pallas_call | solution.py:455
  5.7 2.7 %collective-permute-start.4 = (f32[2,136,128]{2,1,0:T(8,128)S(1)}, f32[2,136,128]{2,1,0:T(8,128)S(1)}, u32[]{:S(2)}, u32[]{:S(2)}) collective-permute-start(f32[2,136,128]{2,1,0:T(8,128)S(1)} %get-tuple-element.23), channel_id=1, source_target_pairs={{0,2},{2,0},{4,6},{6,4},{8,10},{10,8},{12,14},{14,12},{1,3},{3,1},... | collective-permute-start | bytes 417800 | tf_op jit(solution)/shard_map/ppermute | solution.py:471
  8.4 1.3 %collective-permute-start.5 = (f32[2,136,128]{2,1,0:T(8,128)S(1)}, f32[2,136,128]{2,1,0:T(8,128)S(1)}, u32[]{:S(2)}, u32[]{:S(2)}) collective-permute-start(f32[2,136,128]{2,1,0:T(8,128)S(1)} %get-tuple-element.24), channel_id=1, source_target_pairs={{0,4},{2,6},{4,0},{6,2},{8,12},{10,14},{12,8},{14,10},{1,5},{3,7},... | collective-permute-start | bytes 417800 | tf_op jit(solution)/shard_map/ppermute | solution.py:471
  9.7 2.2 %collective-permute-start.6 = (f32[2,136,128]{2,1,0:T(8,128)S(1)}, f32[2,136,128]{2,1,0:T(8,128)S(1)}, u32[]{:S(2)}, u32[]{:S(2)}) collective-permute-start(f32[2,136,128]{2,1,0:T(8,128)S(1)} %get-tuple-element.25), channel_id=1, source_target_pairs={{0,14},{2,12},{4,10},{6,8},{8,6},{10,4},{12,2},{14,0},{1,15},{3,13... | collective-permute-start | bytes 417800 | tf_op jit(solution)/shard_map/ppermute | solution.py:471
  11.9 1.1 %collective-permute-start.7 = (f32[2,136,128]{2,1,0:T(8,128)S(1)}, f32[2,136,128]{2,1,0:T(8,128)S(1)}, u32[]{:S(2)}, u32[]{:S(2)}) collective-permute-start(f32[2,136,128]{2,1,0:T(8,128)S(1)} %get-tuple-element.26), channel_id=1, source_target_pairs={{0,12},{2,14},{4,8},{6,10},{8,4},{10,6},{12,0},{14,2},{1,13},{3,15... | collective-permute-start | bytes 417800 | tf_op jit(solution)/shard_map/ppermute | solution.py:471
  13.0 1.4 %collective-permute-start.8 = (f32[2,136,128]{2,1,0:T(8,128)S(1)}, f32[2,136,128]{2,1,0:T(8,128)S(1)}, u32[]{:S(2)}, u32[]{:S(2)}) collective-permute-start(f32[2,136,128]{2,1,0:T(8,128)S(1)} %get-tuple-element.27), channel_id=1, source_target_pairs={{0,10},{2,8},{4,14},{6,12},{8,2},{10,0},{12,6},{14,4},{1,11},{3,9}... | collective-permute-start | bytes 417800 | tf_op jit(solution)/shard_map/ppermute | solution.py:471
  14.4 1.9 %collective-permute-start.9 = (f32[2,136,128]{2,1,0:T(8,128)S(1)}, f32[2,136,128]{2,1,0:T(8,128)S(1)}, u32[]{:S(2)}, u32[]{:S(2)}) collective-permute-start(f32[2,136,128]{2,1,0:T(8,128)S(1)} %get-tuple-element.28), channel_id=1, source_target_pairs={{0,8},{2,10},{4,12},{6,14},{8,0},{10,2},{12,4},{14,6},{1,9},{3,11}... | collective-permute-start | bytes 417800 | tf_op jit(solution)/shard_map/ppermute | solution.py:471
  16.3 0.8 %collective-permute-start.10 = (f32[2,136,128]{2,1,0:T(8,128)S(1)}, f32[2,136,128]{2,1,0:T(8,128)S(1)}, u32[]{:S(2)}, u32[]{:S(2)}) collective-permute-start(f32[2,136,128]{2,1,0:T(8,128)S(1)} %get-tuple-element.29), channel_id=1, source_target_pairs={{0,6},{2,4},{4,2},{6,0},{8,14},{10,12},{12,10},{14,8},{1,7},{3,5},... | collective-permute-start | bytes 417800 | tf_op jit(solution)/shard_map/ppermute | solution.py:471
  17.1 1.4 %phase.1.refs_9_ = f32[2,4,2,128,128]{4,3,2,1,0:T(8,128)S(1)} custom-call(s32[2]{0:T(128)S(1)} %copy-done.8, s32[2]{0:T(128)S(1)} %collective-permute-done.3.off_other), custom_call_target="tpu_custom_call" | custom-call | flops 10000000 | bytes 1000000 | tf_op jit(solution)/shard_map/phase/pallas_call | solution.py:475
  18.5 2.9 %collective-permute-done.7.refs_4_ = f32[2,136,128]{2,1,0:T(8,128)S(1)} collective-permute-done((f32[2,136,128]{2,1,0:T(8,128)S(1)}, f32[2,136,128]{2,1,0:T(8,128)S(1)}, u32[]{:S(2)}, u32[]{:S(2)}) %collective-permute-start.7) | collective-permute-done | bytes 139296 | tf_op jit(solution)/shard_map/ppermute | solution.py:471
  21.4 12.1 %collective-permute-done.8.refs_5_ = f32[2,136,128]{2,1,0:T(8,128)S(1)} collective-permute-done((f32[2,136,128]{2,1,0:T(8,128)S(1)}, f32[2,136,128]{2,1,0:T(8,128)S(1)}, u32[]{:S(2)}, u32[]{:S(2)}) %collective-permute-start.8) | collective-permute-done | bytes 139296 | tf_op jit(solution)/shard_map/ppermute | solution.py:471
  33.4 3.0 %collective-permute-done.9.refs_6_ = f32[2,136,128]{2,1,0:T(8,128)S(1)} collective-permute-done((f32[2,136,128]{2,1,0:T(8,128)S(1)}, f32[2,136,128]{2,1,0:T(8,128)S(1)}, u32[]{:S(2)}, u32[]{:S(2)}) %collective-permute-start.9) | collective-permute-done | bytes 139296 | tf_op jit(solution)/shard_map/ppermute | solution.py:471
  36.5 1.5 %spectrum.2.refs_0_ = f32[4,2,128,128]{3,2,1,0:T(8,128)S(1)} custom-call(f32[2,136,128]{2,1,0:T(8,128)S(1)} %get-tuple-element.22.refs_0_, f32[2,136,128]{2,1,0:T(8,128)S(1)} %collective-permute-done.4.refs_1_, f32[2,136,128]{2,1,0:T(8,128)S(1)} %collective-permute-done.5.refs_2_, f32[2,136,128]{2,1,0:T(8,128)S(1)} %collective-permute-done.6.refs_3_, ...), custom_call_target="tpu_custom_call" | custom-call | flops 400000000 | bytes 2000000 | tf_op jit(solution)/shard_map/spectrum/pallas_call | solution.py:486
  38.0 1.2 %collective-permute-start.11 = (f32[4,2,128,128]{3,2,1,0:T(8,128)S(1)}, f32[4,2,128,128]{3,2,1,0:T(8,128)}, u32[]{:S(2)}, u32[]{:S(2)}) collective-permute-start(f32[4,2,128,128]{3,2,1,0:T(8,128)S(1)} %spectrum.2.refs_0_), channel_id=1, source_target_pairs={{0,1},{1,0},{2,3},{3,2},{4,5},{5,4},{6,7},{7,6},{8,9},{9,8},{10,11... | collective-permute-start | bytes 1572872 | tf_op jit(solution)/shard_map/ppermute | solution.py:501
  39.3 1.4 %spectrum.3.refs_1_ = f32[4,2,128,128]{3,2,1,0:T(8,128)S(1)} custom-call(f32[2,136,128]{2,1,0:T(8,128)S(1)} %get-tuple-element.22.refs_0_, f32[2,136,128]{2,1,0:T(8,128)S(1)} %collective-permute-done.4.refs_1_, f32[2,136,128]{2,1,0:T(8,128)S(1)} %collective-permute-done.5.refs_2_, f32[2,136,128]{2,1,0:T(8,128)S(1)} %collective-permute-done.6.refs_3_, ...), custom_call_target="tpu_custom_call" | custom-call | flops 400000000 | bytes 2000000 | tf_op jit(solution)/shard_map/spectrum/pallas_call | solution.py:486
  40.9 2.2 %image.1 = (f32[128,128]{1,0:T(8,128)S(1)}, f32[128,128]{1,0:T(8,128)S(1)}, f32[128,128]{1,0:T(8,128)S(1)}, f32[128,128]{1,0:T(8,128)S(1)}, f32[128,128]{1,0:T(8...) custom-call(f32[4,2,128,128]{3,2,1,0:T(8,128)S(1)} %spectrum.2.refs_0_, ...), custom_call_target="tpu_custom_call" | custom-call | flops 400000000 | bytes 2000000 | tf_op jit(solution)/shard_map/image/pallas_call | solution.py:504
  43.0 1.9 %collective-permute-start.13 = (f32[128,128]{1,0:T(8,128)S(1)}, f32[128,128]{1,0:T(8,128)S(1)}, u32[]{:S(2)}, u32[]{:S(2)}) collective-permute-start(f32[128,128]{1,0:T(8,128)S(1)} %get-tuple-element.30), channel_id=1, source_target_pairs={{0,0},{1,8},{2,2},{3,10},{4,4},{5,12},{6,6},{7,14},{8,9},{9,1},{10... | collective-permute-start | bytes 196616 | tf_op jit(solution)/shard_map/ppermute | solution.py:527
  45.0 3.8 %collective-permute-start.15 = (f32[128,128]{1,0:T(8,128)S(1)}, f32[128,128]{1,0:T(8,128)S(1)}, u32[]{:S(2)}, u32[]{:S(2)}) collective-permute-start(f32[128,128]{1,0:T(8,128)S(1)} %get-tuple-element.32), channel_id=1, source_target_pairs={{0,4},{1,12},{2,6},{3,14},{4,0},{5,8},{6,2},{7,10},{8,13},{9,5},{1... | collective-permute-start | bytes 196616 | tf_op jit(solution)/shard_map/ppermute | solution.py:527
  48.8 0.9 %collective-permute-start.16 = (f32[128,128]{1,0:T(8,128)S(1)}, f32[128,128]{1,0:T(8,128)S(1)}, u32[]{:S(2)}, u32[]{:S(2)}) collective-permute-start(f32[128,128]{1,0:T(8,128)S(1)} %get-tuple-element.33), channel_id=1, source_target_pairs={{0,6},{1,14},{2,4},{3,12},{4,2},{5,10},{6,0},{7,8},{8,15},{9,7},{1... | collective-permute-start | bytes 196616 | tf_op jit(solution)/shard_map/ppermute | solution.py:527
  49.8 1.9 %collective-permute-start.17 = (f32[128,128]{1,0:T(8,128)S(1)}, f32[128,128]{1,0:T(8,128)S(1)}, u32[]{:S(2)}, u32[]{:S(2)}) collective-permute-start(f32[128,128]{1,0:T(8,128)S(1)} %get-tuple-element.34), channel_id=1, source_target_pairs={{0,8},{1,0},{2,10},{3,2},{4,12},{5,4},{6,14},{7,6},{8,1},{9,9},{10... | collective-permute-start | bytes 196616 | tf_op jit(solution)/shard_map/ppermute | solution.py:527
  51.7 3.2 %collective-permute-start.18 = (f32[128,128]{1,0:T(8,128)S(1)}, f32[128,128]{1,0:T(8,128)S(1)}, u32[]{:S(2)}, u32[]{:S(2)}) collective-permute-start(f32[128,128]{1,0:T(8,128)S(1)} %get-tuple-element.35), channel_id=1, source_target_pairs={{0,10},{1,2},{2,8},{3,0},{4,14},{5,6},{6,12},{7,4},{8,3},{9,11},{1... | collective-permute-start | bytes 196616 | tf_op jit(solution)/shard_map/ppermute | solution.py:527
  54.9 2.6 %collective-permute-start.19 = (f32[128,128]{1,0:T(8,128)S(1)}, f32[128,128]{1,0:T(8,128)S(1)}, u32[]{:S(2)}, u32[]{:S(2)}) collective-permute-start(f32[128,128]{1,0:T(8,128)S(1)} %get-tuple-element.36), channel_id=1, source_target_pairs={{0,12},{1,4},{2,14},{3,6},{4,8},{5,0},{6,10},{7,2},{8,5},{9,13},{1... | collective-permute-start | bytes 196616 | tf_op jit(solution)/shard_map/ppermute | solution.py:527
  57.6 2.9 %collective-permute-done.19.refs_6_ = f32[128,128]{1,0:T(8,128)S(1)} collective-permute-done((f32[128,128]{1,0:T(8,128)S(1)}, f32[128,128]{1,0:T(8,128)S(1)}, u32[]{:S(2)}, u32[]{:S(2)}) %collective-permute-start.19) | collective-permute-done | bytes 65568 | tf_op jit(solution)/shard_map/ppermute | solution.py:527
  60.5 3.5 %collective-permute-done.20.refs_7_ = f32[128,128]{1,0:T(8,128)S(1)} collective-permute-done((f32[128,128]{1,0:T(8,128)S(1)}, f32[128,128]{1,0:T(8,128)S(1)}, u32[]{:S(2)}, u32[]{:S(2)}) %collective-permute-start.20) | collective-permute-done | bytes 65568 | tf_op jit(solution)/shard_map/ppermute | solution.py:527
  63.9 0.9 %place.1 = (f32[32,2048]{1,0:T(8,128)}, f32[32,2048]{1,0:T(8,128)}) custom-call(f32[128,128]{1,0:T(8,128)S(1)} %collective-permute-done.13.refs_0_, f32[128,128]{1,0:T(8,128)S(1)} %collective-permute-done.14.refs_1_, f32[128,128]{1,0:T(8,128)S(1)} %collective-permute-done.15.refs_2_, f32[128,128]{1,0:T(8,128)S(1)} %collective-permute-done.16.refs_3_, ...), custom_call_target="tpu_custom_call" | custom-call | bytes 1000000 | tf_op jit(solution)/shard_map/place/pallas_call | solution.py:528
  (41 shorter events, 0.6 us)
Async XLA Ops:
  0.6 4.2 %collective-permute-start = (f32[32,2048]{1,0:T(8,128)}, f32[32,2048]{1,0:T(8,128)S(1)}, u32[]{:S(2)}, u32[]{:S(2)}) collective-permute-start(f32[32,2048]{1,0:T(8,128)} %re_own.1), channel_id=1, source_target_pairs={{0,1},{1,0},{2,3},{3,2},{4,5},{5,4},{6,7},{7,6},{8,9},{9,8},{10,11... | collective-permute-start | bytes 786440 | tf_op jit(solution)/shard_map/ppermute | solution.py:442
  0.8 4.1 %collective-permute-start.1 = (f32[32,2048]{1,0:T(8,128)}, f32[32,2048]{1,0:T(8,128)S(1)}, u32[]{:S(2)}, u32[]{:S(2)}) collective-permute-start(f32[32,2048]{1,0:T(8,128)} %im_own.1), channel_id=1, source_target_pairs={{0,1},{1,0},{2,3},{3,2},{4,5},{5,4},{6,7},{7,6},{8,9},{9,8},{10,11... | collective-permute-start | bytes 786440 | tf_op jit(solution)/shard_map/ppermute | solution.py:442
  2.0 0.7 %copy-start.8 = (s32[2]{0:T(128)S(1)}, s32[2]{0:T(128)}, u32[]{:S(2)}) copy-start(s32[2]{0:T(128)} %off_own.3) | copy-start | bytes 28
  2.0 2.8 %collective-permute-start.2 = (f32[64,32]{1,0:T(8,128)S(1)}, f32[64,32]{1,0:T(8,128)S(1)}, u32[]{:S(2)}, u32[]{:S(2)}) collective-permute-start(f32[64,32]{1,0:T(8,128)S(1)} %bitcast.1), channel_id=1, source_target_pairs={{0,1},{1,0},{2,3},{3,2},{4,5},{5,4},{6,7},{7,6},{8,9},{9,8},{10,11... | collective-permute-start | bytes 24584 | tf_op jit(solution)/shard_map/ppermute | solution.py:442
  2.7 2.1 %collective-permute-start.3 = (s32[2]{0:T(128)S(1)}, s32[2]{0:T(128)S(1)}, u32[]{:S(2)}, u32[]{:S(2)}) collective-permute-start(s32[2]{0:T(128)S(1)} %copy-done.8), channel_id=1, source_target_pairs={{0,1},{1,0},{2,3},{3,2},{4,5},{5,4},{6,7},{7,6},{8,9},{9,8},{10,11... | collective-permute-start | bytes 32 | tf_op jit(solution)/shard_map/ppermute | solution.py:441
  2.7 0.9 %copy-start.6 = (f32[32,2048]{1,0:T(8,128)S(1)}, f32[32,2048]{1,0:T(8,128)}, u32[]{:S(2)}) copy-start(f32[32,2048]{1,0:T(8,128)} %re_own.1) | copy-start | bytes 786436
  3.7 0.9 %copy-start.7 = (f32[32,2048]{1,0:T(8,128)S(1)}, f32[32,2048]{1,0:T(8,128)}, u32[]{:S(2)}) copy-start(f32[32,2048]{1,0:T(8,128)} %im_own.1) | copy-start | bytes 786436
  5.7 8.7 %collective-permute-start.4 = (f32[2,136,128]{2,1,0:T(8,128)S(1)}, f32[2,136,128]{2,1,0:T(8,128)S(1)}, u32[]{:S(2)}, u32[]{:S(2)}) collective-permute-start(f32[2,136,128]{2,1,0:T(8,128)S(1)} %get-tuple-element.23), channel_id=1, source_target_pairs={{0,2},{2,0},{4,6},{6,4},{8,10},{10,8},{12,14},{14,12},{1,3},{3,1},... | collective-permute-start | bytes 417800 | tf_op jit(solution)/shard_map/ppermute | solution.py:471
  8.4 7.8 %collective-permute-start.5 = (f32[2,136,128]{2,1,0:T(8,128)S(1)}, f32[2,136,128]{2,1,0:T(8,128)S(1)}, u32[]{:S(2)}, u32[]{:S(2)}) collective-permute-start(f32[2,136,128]{2,1,0:T(8,128)S(1)} %get-tuple-element.24), channel_id=1, source_target_pairs={{0,4},{2,6},{4,0},{6,2},{8,12},{10,14},{12,8},{14,10},{1,5},{3,7},... | collective-permute-start | bytes 417800 | tf_op jit(solution)/shard_map/ppermute | solution.py:471
  9.7 8.8 %collective-permute-start.6 = (f32[2,136,128]{2,1,0:T(8,128)S(1)}, f32[2,136,128]{2,1,0:T(8,128)S(1)}, u32[]{:S(2)}, u32[]{:S(2)}) collective-permute-start(f32[2,136,128]{2,1,0:T(8,128)S(1)} %get-tuple-element.25), channel_id=1, source_target_pairs={{0,14},{2,12},{4,10},{6,8},{8,6},{10,4},{12,2},{14,0},{1,15},{3,13... | collective-permute-start | bytes 417800 | tf_op jit(solution)/shard_map/ppermute | solution.py:471
  11.9 9.5 %collective-permute-start.7 = (f32[2,136,128]{2,1,0:T(8,128)S(1)}, f32[2,136,128]{2,1,0:T(8,128)S(1)}, u32[]{:S(2)}, u32[]{:S(2)}) collective-permute-start(f32[2,136,128]{2,1,0:T(8,128)S(1)} %get-tuple-element.26), channel_id=1, source_target_pairs={{0,12},{2,14},{4,8},{6,10},{8,4},{10,6},{12,0},{14,2},{1,13},{3,15... | collective-permute-start | bytes 417800 | tf_op jit(solution)/shard_map/ppermute | solution.py:471
  13.0 20.5 %collective-permute-start.8 = (f32[2,136,128]{2,1,0:T(8,128)S(1)}, f32[2,136,128]{2,1,0:T(8,128)S(1)}, u32[]{:S(2)}, u32[]{:S(2)}) collective-permute-start(f32[2,136,128]{2,1,0:T(8,128)S(1)} %get-tuple-element.27), channel_id=1, source_target_pairs={{0,10},{2,8},{4,14},{6,12},{8,2},{10,0},{12,6},{14,4},{1,11},{3,9}... | collective-permute-start | bytes 417800 | tf_op jit(solution)/shard_map/ppermute | solution.py:471
  14.4 22.0 %collective-permute-start.9 = (f32[2,136,128]{2,1,0:T(8,128)S(1)}, f32[2,136,128]{2,1,0:T(8,128)S(1)}, u32[]{:S(2)}, u32[]{:S(2)}) collective-permute-start(f32[2,136,128]{2,1,0:T(8,128)S(1)} %get-tuple-element.28), channel_id=1, source_target_pairs={{0,8},{2,10},{4,12},{6,14},{8,0},{10,2},{12,4},{14,6},{1,9},{3,11}... | collective-permute-start | bytes 417800 | tf_op jit(solution)/shard_map/ppermute | solution.py:471
  16.3 20.2 %copy-start = (bf16[256,256]{1,0:T(8,128)(2,1)S(1)}, bf16[256,256]{1,0:T(8,128)(2,1)}, u32[]{:S(2)}) copy-start(bf16[256,256]{1,0:T(8,128)(2,1)} %constant.12.clone.refs_10_.refs_5_) | copy-start | bytes 393220
  16.3 20.2 %copy-start.1 = (bf16[256,256]{1,0:T(8,128)(2,1)S(1)}, bf16[256,256]{1,0:T(8,128)(2,1)}, u32[]{:S(2)}) copy-start(bf16[256,256]{1,0:T(8,128)(2,1)} %constant.13.clone.refs_11_.refs_6_) | copy-start | bytes 393220
  16.3 20.2 %copy-start.2 = (bf16[256,256]{1,0:T(8,128)(2,1)S(1)}, bf16[256,256]{1,0:T(8,128)(2,1)}, u32[]{:S(2)}) copy-start(bf16[256,256]{1,0:T(8,128)(2,1)} %constant.14.clone.refs_12_.refs_7_) | copy-start | bytes 393220
  16.3 20.2 %copy-start.3 = (bf16[256,256]{1,0:T(8,128)(2,1)S(1)}, bf16[256,256]{1,0:T(8,128)(2,1)}, u32[]{:S(2)}) copy-start(bf16[256,256]{1,0:T(8,128)(2,1)} %constant.15.clone.refs_13_.refs_8_) | copy-start | bytes 393220
  16.3 20.2 %copy-start.4 = (f32[128,128]{1,0:T(8,128)S(1)}, f32[128,128]{1,0:T(8,128)}, u32[]{:S(2)}) copy-start(f32[128,128]{1,0:T(8,128)} %constant.16.clone.refs_14_.refs_9_) | copy-start | bytes 196612
  16.3 20.2 %copy-start.5 = (f32[128,128]{1,0:T(8,128)S(1)}, f32[128,128]{1,0:T(8,128)}, u32[]{:S(2)}) copy-start(f32[128,128]{1,0:T(8,128)} %constant.17.clone.refs_15_.refs_10_) | copy-start | bytes 196612
  16.3 20.1 %collective-permute-start.10 = (f32[2,136,128]{2,1,0:T(8,128)S(1)}, f32[2,136,128]{2,1,0:T(8,128)S(1)}, u32[]{:S(2)}, u32[]{:S(2)}) collective-permute-start(f32[2,136,128]{2,1,0:T(8,128)S(1)} %get-tuple-element.29), channel_id=1, source_target_pairs={{0,6},{2,4},{4,2},{6,0},{8,14},{10,12},{12,10},{14,8},{1,7},{3,5},... | collective-permute-start | bytes 417800 | tf_op jit(solution)/shard_map/ppermute | solution.py:471
  18.5 18.0 %copy-start.9 = (s32[2]{0:T(128)S(1)}, s32[2]{0:T(128)}, u32[]{:S(2)}) copy-start(s32[2]{0:T(128)} %refs_8_.4) | copy-start | bytes 28
  36.5 2.7 %copy-start.10 = (f32[32,8]{0,1:T(8,128)S(1)}, f32[32,8]{0,1:T(8,128)}, u32[]{:S(2)}) copy-start(f32[32,8]{0,1:T(8,128)} %param.17) | copy-start | bytes 3076
  38.0 2.9 %collective-permute-start.11 = (f32[4,2,128,128]{3,2,1,0:T(8,128)S(1)}, f32[4,2,128,128]{3,2,1,0:T(8,128)}, u32[]{:S(2)}, u32[]{:S(2)}) collective-permute-start(f32[4,2,128,128]{3,2,1,0:T(8,128)S(1)} %spectrum.2.refs_0_), channel_id=1, source_target_pairs={{0,1},{1,0},{2,3},{3,2},{4,5},{5,4},{6,7},{7,6},{8,9},{9,8},{10,11... | collective-permute-start | bytes 1572872 | tf_op jit(solution)/shard_map/ppermute | solution.py:501
  39.3 1.5 %collective-permute-start.12 = (f32[32,8]{1,0:T(8,128)S(1)}, f32[32,8]{1,0:T(8,128)S(1)}, u32[]{:S(2)}, u32[]{:S(2)}) collective-permute-start(f32[32,8]{1,0:T(8,128)S(1)} %copy.16.refs_3_), channel_id=1, source_target_pairs={{0,1},{1,0},{2,3},{3,2},{4,5},{5,4},{6,7},{7,6},{8,9},{9,8},{10,11... | collective-permute-start | bytes 3080 | tf_op jit(solution)/shard_map/ppermute | solution.py:442
  43.0 8.6 %collective-permute-start.13 = (f32[128,128]{1,0:T(8,128)S(1)}, f32[128,128]{1,0:T(8,128)S(1)}, u32[]{:S(2)}, u32[]{:S(2)}) collective-permute-start(f32[128,128]{1,0:T(8,128)S(1)} %get-tuple-element.30), channel_id=1, source_target_pairs={{0,0},{1,8},{2,2},{3,10},{4,4},{5,12},{6,6},{7,14},{8,9},{9,1},{10... | collective-permute-start | bytes 196616 | tf_op jit(solution)/shard_map/ppermute | solution.py:527
  45.0 9.9 %collective-permute-start.14 = (f32[128,128]{1,0:T(8,128)S(1)}, f32[128,128]{1,0:T(8,128)S(1)}, u32[]{:S(2)}, u32[]{:S(2)}) collective-permute-start(f32[128,128]{1,0:T(8,128)S(1)} %get-tuple-element.31), channel_id=1, source_target_pairs={{0,2},{1,10},{2,0},{3,8},{4,6},{5,14},{6,4},{7,12},{8,11},{9,3},{1... | collective-permute-start | bytes 196616 | tf_op jit(solution)/shard_map/ppermute | solution.py:527
  45.0 12.5 %collective-permute-start.15 = (f32[128,128]{1,0:T(8,128)S(1)}, f32[128,128]{1,0:T(8,128)S(1)}, u32[]{:S(2)}, u32[]{:S(2)}) collective-permute-start(f32[128,128]{1,0:T(8,128)S(1)} %get-tuple-element.32), channel_id=1, source_target_pairs={{0,4},{1,12},{2,6},{3,14},{4,0},{5,8},{6,2},{7,10},{8,13},{9,5},{1... | collective-permute-start | bytes 196616 | tf_op jit(solution)/shard_map/ppermute | solution.py:527
  48.8 8.8 %collective-permute-start.16 = (f32[128,128]{1,0:T(8,128)S(1)}, f32[128,128]{1,0:T(8,128)S(1)}, u32[]{:S(2)}, u32[]{:S(2)}) collective-permute-start(f32[128,128]{1,0:T(8,128)S(1)} %get-tuple-element.33), channel_id=1, source_target_pairs={{0,6},{1,14},{2,4},{3,12},{4,2},{5,10},{6,0},{7,8},{8,15},{9,7},{1... | collective-permute-start | bytes 196616 | tf_op jit(solution)/shard_map/ppermute | solution.py:527
  49.8 7.8 %collective-permute-start.17 = (f32[128,128]{1,0:T(8,128)S(1)}, f32[128,128]{1,0:T(8,128)S(1)}, u32[]{:S(2)}, u32[]{:S(2)}) collective-permute-start(f32[128,128]{1,0:T(8,128)S(1)} %get-tuple-element.34), channel_id=1, source_target_pairs={{0,8},{1,0},{2,10},{3,2},{4,12},{5,4},{6,14},{7,6},{8,1},{9,9},{10... | collective-permute-start | bytes 196616 | tf_op jit(solution)/shard_map/ppermute | solution.py:527
  51.7 5.9 %collective-permute-start.18 = (f32[128,128]{1,0:T(8,128)S(1)}, f32[128,128]{1,0:T(8,128)S(1)}, u32[]{:S(2)}, u32[]{:S(2)}) collective-permute-start(f32[128,128]{1,0:T(8,128)S(1)} %get-tuple-element.35), channel_id=1, source_target_pairs={{0,10},{1,2},{2,8},{3,0},{4,14},{5,6},{6,12},{7,4},{8,3},{9,11},{1... | collective-permute-start | bytes 196616 | tf_op jit(solution)/shard_map/ppermute | solution.py:527
  54.9 5.6 %collective-permute-start.19 = (f32[128,128]{1,0:T(8,128)S(1)}, f32[128,128]{1,0:T(8,128)S(1)}, u32[]{:S(2)}, u32[]{:S(2)}) collective-permute-start(f32[128,128]{1,0:T(8,128)S(1)} %get-tuple-element.36), channel_id=1, source_target_pairs={{0,12},{1,4},{2,14},{3,6},{4,8},{5,0},{6,10},{7,2},{8,5},{9,13},{1... | collective-permute-start | bytes 196616 | tf_op jit(solution)/shard_map/ppermute | solution.py:527
  57.5 6.4 %collective-permute-start.20 = (f32[128,128]{1,0:T(8,128)S(1)}, f32[128,128]{1,0:T(8,128)S(1)}, u32[]{:S(2)}, u32[]{:S(2)}) collective-permute-start(f32[128,128]{1,0:T(8,128)S(1)} %get-tuple-element.37), channel_id=1, source_target_pairs={{0,14},{1,6},{2,12},{3,4},{4,10},{5,2},{6,8},{7,0},{8,7},{9,15},{1... | collective-permute-start | bytes 196616 | tf_op jit(solution)/shard_map/ppermute | solution.py:527

commit v3 on v2

--- a/solution.py
+++ b/solution.py
@@ -164,7 +164,8 @@
 
 FACTOR = 128
 GROUP = 4
-WINDOW = 4 * GROUP
+WINDOW = 2 * GROUP + TAPS - 1
+REF_LINES = 8
 EDGE = 16
 
 
@@ -256,24 +257,24 @@
     ref_rows = ref_own.shape[0]
     row = lax.broadcasted_iota(jnp.int32, (ref_rows, FACTOR), 0)
     column = lax.broadcasted_iota(jnp.int32, (ref_rows, FACTOR), 1)
-    spread = (column * ref_rows // FACTOR == row).astype(jnp.float32)
+    twice = (lax.rem(column, ref_rows) == row).astype(jnp.float32)
     ref_all[:EDGE, :] = jnp.zeros((EDGE, FACTOR), jnp.float32)
     ref_all[EDGE + 2 * bins :, :] = jnp.zeros((EDGE, FACTOR), jnp.float32)
     for at, ref in ((own_at, ref_own), (other_at, ref_other)):
         ref_all[pl.ds(pl.multiple_of(at, 16), bins), :] = lax.dot_general(
-            ref[...], spread, (((0,), (0,)), ((), ())), precision=PRECISE, preferred_element_type=jnp.float32
+            ref[...], twice, (((0,), (0,)), ((), ())), precision=PRECISE, preferred_element_type=jnp.float32
         )
-    body = GROUP * part_rows
+    body = WINDOW * part_rows
+    lane = lax.broadcasted_iota(jnp.int32, (1, FACTOR), 1)
     for step, message in enumerate(messages):
-        chip = place ^ step
-        start = window_start(chip, side, off_own, off_other) + EDGE
-        for group, group_at in enumerate(group_starts(side)):
-            rows = pl.ds(pl.multiple_of((start + group_at) * part_rows, 8), body)
-            message[group, :body, :] = re_all[rows, :]
-            message[group, body : 2 * body, :] = im_all[rows, :]
-            for bin_num in range(GROUP):
-                message[group, 2 * body + bin_num, :] = ref_all[start + group_at + bin_num, :]
-            message[group, 2 * body + GROUP :, :] = jnp.zeros((8 - GROUP, FACTOR), jnp.float32)
+        start = window_start(((place >> 1) ^ step) * 2 + side, side, off_own, off_other) + EDGE
+        rows = pl.ds(pl.multiple_of(start * part_rows, 8), body)
+        message[:body, :] = re_all[rows, :]
+        message[body : 2 * body, :] = im_all[rows, :]
+        for bin_num in range(REF_LINES):
+            low = ref_all[pl.ds(start + bin_num, 1), :]
+            high = ref_all[pl.ds(start + REF_LINES + bin_num, 1), :]
+            message[2 * body + bin_num : 2 * body + bin_num + 1, :] = jnp.where(lane < FACTOR // 2, low, high)
 
 
 def phase_kernel(bins_total, off_own, off_other, out):
@@ -296,22 +297,36 @@
             out[group, bin_num, 1] = sine
 
 
-def spectrum_body(steps, group, *refs):
-    places = len(steps)
+def spectrum_body(places, group, *refs):
     chunks, refs = refs[:places], refs[places:]
-    owners, phase, high1, low1, high2, low2, twist_cos, twist_sin, out, lines, picks = refs
-    place = lax.axis_index("az")
+    owners, phase, high1, low1, high2, low2, twist_cos, twist_sin, out, lines, picks, picked = refs
+    place, side = lax.axis_index("az"), lax.axis_index("rg")
     samples = FACTOR * FACTOR // places
     part_rows = samples // FACTOR
-    for step, chunk in zip(steps, chunks):
-        source = place ^ step
-        for line in range(2 * GROUP):
-            at = pl.multiple_of(line * FACTOR + source * part_rows, 8)
-            lines[pl.ds(at, part_rows), :] = chunk[group, line * part_rows : (line + 1) * part_rows, :]
-        picks[source] = chunk[group, 2 * GROUP * part_rows :, :]
-    lane = lax.broadcasted_iota(jnp.int32, (2 * GROUP, FACTOR), 1)
-    ref_phase = jnp.where(lane < FACTOR // 2, picks[owners[1]], picks[owners[0]])
-    ref_cos, ref_sin = cos_sin_quarters(ref_phase * (2 / math.pi))
+    body = WINDOW * part_rows
+    start = group_starts(side)[group]
+    for at, chunk in enumerate(chunks):
+        source = ((place >> 1) ^ (at // 2)) * 2 + (side if at % 2 == 0 else 1 - side)
+        for part in range(2):
+            for bin_num in range(GROUP):
+                row = jnp.minimum(start + bin_num, WINDOW - 1)
+                read = pl.multiple_of(part * body + row * part_rows, 8)
+                write = pl.multiple_of((part * GROUP + bin_num) * FACTOR + source * part_rows, 8)
+                lines[pl.ds(write, part_rows), :] = chunk[pl.ds(read, part_rows), :]
+        picks[source] = chunk[2 * body :, :]
+    row = lax.broadcasted_iota(jnp.int32, (FACTOR, FACTOR), 0)
+    column = lax.broadcasted_iota(jnp.int32, (FACTOR, FACTOR), 1)
+    lane = lax.broadcasted_iota(jnp.int32, (REF_LINES, FACTOR), 1)
+    for block in range(2):
+        spread = (row == column // 2 + block * (FACTOR // 2)).astype(jnp.float32)
+        wide = [
+            jnp.dot(picks[owners[which]], spread, precision=PRECISE, preferred_element_type=jnp.float32)
+            for which in range(2)
+        ]
+        ref_phase = jnp.where(lane < FACTOR // 2, wide[1], wide[0])
+        ref_cos, ref_sin = cos_sin_quarters(ref_phase * (2 / math.pi))
+        picked[0, block * REF_LINES : (block + 1) * REF_LINES, :] = ref_cos
+        picked[1, block * REF_LINES : (block + 1) * REF_LINES, :] = ref_sin
     first, second = (high1[...], low1[...]), (high2[...], low2[...])
     for pair in range(GROUP // 2):
         bins = (2 * pair, 2 * pair + 1)
@@ -333,7 +348,7 @@
             real = passed[at * FACTOR : (at + 1) * FACTOR, :FACTOR]
             imag = passed[at * FACTOR : (at + 1) * FACTOR, FACTOR:]
             model_cos, model_sin = phase[group, bin_num, 0], phase[group, bin_num, 1]
-            row_cos, row_sin = ref_cos[bin_num : bin_num + 1, :], ref_sin[bin_num : bin_num + 1, :]
+            row_cos, row_sin = picked[0, pl.ds(start + bin_num, 1), :], picked[1, pl.ds(start + bin_num, 1), :]
             cosine = model_cos * row_cos - model_sin * row_sin
             sine = model_sin * row_cos + model_cos * row_sin
             out[bin_num, 0] = real * cosine - imag * sine
@@ -342,7 +357,7 @@
 
 def image_kernel(places, *refs):
     shared, kept, received, taps_own, taps_other, high1, low1, high2, low2, twist_cos, twist_sin = refs[:11]
-    messages, (band, lines) = refs[11:-2], refs[-2:]
+    give, keep, band, lines = refs[11:]
     place, side = lax.axis_index("az"), lax.axis_index("rg")
     samples = FACTOR * FACTOR // places
     part_rows = samples // FACTOR
@@ -392,11 +407,19 @@
                 lines[(part * GROUP + bin_num) * FACTOR : (part * GROUP + bin_num + 1) * FACTOR, :] = passed[
                     part * FACTOR : (part + 1) * FACTOR, at * FACTOR : (at + 1) * FACTOR
                 ]
+    for pair in range(places // 2):
+        for piece, core in ((give, 1 - side), (keep, side)):
+            for line in range(2 * GROUP):
+                at = pl.multiple_of(line * FACTOR + (2 * pair + core) * part_rows, 8)
+                piece[pair, line * part_rows : (line + 1) * part_rows, :] = lines[pl.ds(at, part_rows), :]
+
+
+def merge_kernel(half, keep, got, *messages):
+    quarter = lax.rem(lax.axis_index("az"), half)
+    size = keep.shape[1]
     for step, message in enumerate(messages):
-        chip = place ^ step ^ (side * (places // 2))
-        for line in range(2 * GROUP):
-            at = pl.multiple_of(line * FACTOR + chip * part_rows, 8)
-            message[line * part_rows : (line + 1) * part_rows, :] = lines[pl.ds(at, part_rows), :]
+        message[:size, :] = keep[quarter ^ step]
+        message[size:, :] = got[quarter ^ step]
 
 
 def place_kernel(*refs):
@@ -404,14 +427,14 @@
     bins, samples = out_re.shape
     part_rows = samples // FACTOR
     body = GROUP * part_rows
-    half = len(messages) // 2
-    place, side = lax.axis_index("az"), lax.axis_index("rg")
+    place = lax.axis_index("az")
+    core = place & 1
     for step, message in enumerate(messages):
-        chip = place ^ step
-        core = (lax.div(chip, half) != side).astype(jnp.int32)
-        at = pl.multiple_of((lax.rem(chip, half) * 2 + core) * body, 8)
-        re_all[pl.ds(at, body), :] = message[:body, :]
-        im_all[pl.ds(at, body), :] = message[body:, :]
+        sender = (place >> 1) ^ step
+        for which in range(2):
+            at = pl.multiple_of((sender * 2 + (core if which == 0 else 1 - core)) * body, 8)
+            re_all[pl.ds(at, body), :] = message[2 * which * body : (2 * which + 1) * body, :]
+            im_all[pl.ds(at, body), :] = message[(2 * which + 1) * body : (2 * which + 2) * body, :]
     for out, all_ref in ((out_re, re_all), (out_im, im_all)):
         for tile in range(0, bins, 8):
             for row in range(part_rows):
@@ -442,7 +465,8 @@
     ref_other, re_other, im_other, taps_other = swap(ref_own), swap(raw_re), swap(raw_im), swap(taps)
 
     part_rows = samples // FACTOR
-    message = jax.ShapeDtypeStruct((2, 2 * GROUP * part_rows + 8, FACTOR), f32)
+    half = places // 2
+    message = jax.ShapeDtypeStruct((2 * WINDOW * part_rows + REF_LINES, FACTOR), f32)
     lines = pl.pallas_call(
         spread_kernel,
         out_shape=[jax.ShapeDtypeStruct((bins * part_rows, FACTOR), f32)] * 2,
@@ -454,9 +478,9 @@
     )(raw_re, raw_im)
     messages = pl.pallas_call(
         pack_kernel,
-        out_shape=[message] * places,
+        out_shape=[message] * half,
         in_specs=[VMEM] * 6 + [SMEM] * 2,
-        out_specs=[VMEM] * places,
+        out_specs=[VMEM] * half,
         scratch_shapes=[
             pltpu.VMEM(((2 * bins + 2 * EDGE) * part_rows, FACTOR), f32),
             pltpu.VMEM(((2 * bins + 2 * EDGE) * part_rows, FACTOR), f32),
@@ -466,11 +490,15 @@
         cost_estimate=cost(10**6, 4 * 10**6),
         name="pack",
     )(*lines, re_other, im_other, ref_own, ref_other, offsets, offsets_other)
-    steps = (0, 1, 2, 7, 6, 5, 4, 3)
-    chunks = [
-        lax.ppermute(messages[step], "az", [(i, i ^ step) for i in range(places)]) if step else messages[step]
-        for step in steps
-    ]
+    chunks = [None] * places
+    for step in reversed(range(half)):
+        route = [
+            (chip * 2 + core, (((chip >> 1) ^ step) * 2 + core) * 2 + (chip & 1))
+            for chip in range(places)
+            for core in range(2)
+        ]
+        chunks[2 * step] = lax.ppermute(messages[step], ("az", "rg"), route)
+        chunks[2 * step + 1] = swap(chunks[2 * step])
 
     phases = pl.pallas_call(
         functools.partial(phase_kernel, 2 * bins),
@@ -484,13 +512,14 @@
 
     def spectrum(group):
         return pl.pallas_call(
-            functools.partial(spectrum_body, steps, group),
+            functools.partial(spectrum_body, places, group),
             out_shape=jax.ShapeDtypeStruct((GROUP, 2, FACTOR, FACTOR), f32),
             in_specs=[VMEM] * places + [SMEM] + [VMEM] * 7,
             out_specs=VMEM,
             scratch_shapes=[
                 pltpu.VMEM((2 * GROUP * FACTOR, FACTOR), f32),
-                pltpu.VMEM((places, 2 * GROUP, FACTOR), f32),
+                pltpu.VMEM((places, REF_LINES, FACTOR), f32),
+                pltpu.VMEM((2, 2 * REF_LINES, FACTOR), f32),
             ],
             compiler_params=KERNEL,
             cost_estimate=cost(4 * 10**8, 2 * 10**6),
@@ -501,11 +530,12 @@
     received = swap(shared)
     kept = spectrum(1)
 
-    pieces = pl.pallas_call(
+    piece = jax.ShapeDtypeStruct((half, 2 * GROUP * part_rows, FACTOR), f32)
+    give, keep = pl.pallas_call(
         functools.partial(image_kernel, places),
-        out_shape=[jax.ShapeDtypeStruct((2 * GROUP * part_rows, FACTOR), f32)] * places,
+        out_shape=[piece] * 2,
         in_specs=[VMEM] * 3 + [SMEM] * 2 + [VMEM] * 6,
-        out_specs=[VMEM] * places,
+        out_specs=[VMEM] * 2,
         scratch_shapes=[
             pltpu.VMEM((GROUP * FACTOR, 2 * FACTOR), f32),
             pltpu.VMEM((2 * GROUP * FACTOR, FACTOR), f32),
@@ -514,21 +544,29 @@
         cost_estimate=cost(4 * 10**8, 2 * 10**6),
         name="image",
     )(shared, kept, received, taps, taps_other, *matrices, *twists)
-
-    half = places // 2
+    pieces = pl.pallas_call(
+        functools.partial(merge_kernel, half),
+        out_shape=[jax.ShapeDtypeStruct((4 * GROUP * part_rows, FACTOR), f32)] * half,
+        in_specs=[VMEM] * 2,
+        out_specs=[VMEM] * half,
+        compiler_params=KERNEL,
+        cost_estimate=cost(0, 10**6),
+        name="merge",
+    )(keep, swap(give))
+
     routes = [
         [
-            (chip * 2 + core, (chip ^ step ^ (core * half)) * 2 + chip // half)
+            (chip * 2 + core, (((chip % half) ^ step) * 2 + core) * 2 + chip // half)
             for chip in range(places)
             for core in range(2)
         ]
-        for step in range(places)
+        for step in range(half)
     ]
     pieces = [lax.ppermute(piece, ("az", "rg"), route) for piece, route in zip(pieces, routes)]
     return pl.pallas_call(
         place_kernel,
         out_shape=[jax.ShapeDtypeStruct((bins, samples), f32)] * 2,
-        in_specs=[VMEM] * places,
+        in_specs=[VMEM] * half,
         out_specs=[VMEM] * 2,
         scratch_shapes=[pltpu.VMEM((bins * part_rows, FACTOR), f32)] * 2,
         compiler_params=KERNEL,
@@ -547,8 +585,7 @@
             and raw_re.shape[0] == 2 * GROUP * sizes["az"]
             and line == FACTOR * FACTOR
             and line // sizes["az"] % (8 * FACTOR) == 0
-            and ref_blocks.shape[1] <= FACTOR
-            and FACTOR % ref_blocks.shape[1] == 0
+            and ref_blocks.shape[1] == FACTOR // 2
         )
         return jax.shard_map(
             transposed_shards if fits else butterfly_shards,

time: 65.2 us -> 68 us (1.043)
  the two profiles are of different devices: /device:TPU:1 before, /device:TPU:0 now
where the time goes in v3:
time: 68 us; the launch traced here: 67.6 us
  starting transfers between devices  39.7 us (58%)
  waiting for transfers between devices  12.3 us (18%)
  Pallas kernels  8.86 us (13%)
  local copies, waits for them, and re-layouts  5.82 us (9%)
  between operations  0.93 us (1%)
    ppermute x4, starting transfers between devices, transposed_shards(): chunks[2 * step + 1] = swap(chunks[2 * step])  19.3 us
    ppermute x4, starting transfers between devices, transposed_shards(): lax.ppermute(piece, ('az', 'rg'), route)  11.6 us
    ppermute x4, waiting for transfers between devices, transposed_shards(): lax.ppermute(piece, ('az', 'rg'), route)  9.97 us
    ppermute x4, starting transfers between devices, transposed_shards(): chunks[2 * step] = lax.ppermute(messages[step], ('az', 'rg'), route)  6.05 us
    unnamed x36, local copies, waits for them, and re-layouts  5.82 us
    pallas_call x2, Pallas kernels, spectrum(): pl.pallas_call(functools.partial(spectrum_body, places, group), out_shape...  3.26 us
    pallas_call x1, Pallas kernels, transposed_shards(): pl.pallas_call(functools.partial(image_kernel, places), out_shape=[piece]...  2.24 us
    pallas_call x1, Pallas kernels, transposed_shards(): pl.pallas_call(functools.partial(phase_kernel, 2 * bins), out_shape=jax.S...  1.37 us
  transfers between devices with their start and end apart: 19, of which 5 were waited for; matrix products, arithmetic and copies ran while one was open for 1% of the time, Pallas kernels for 5%

profile of v3, /device:TPU:0, one launch (start us, length us, event | category | flops | bytes accessed | tf_op | source)
XLA Modules:
  0.0 67.6 jit_solution(7281212753729663330)
XLA Ops:
  0.6 0.5 collective-permute-start
  1.2 0.8 %copy.14 = f32[1,64,32]{2,1,0:T(8,128)S(1)} copy(f32[1,64,32]{1,2,0:T(8,128)} %param.14) | data formatting | bytes 16384 | tf_op args[2]
  2.0 0.5 collective-permute-start.2
  2.5 0.2 copy-done.14
  2.7 0.4 collective-permute-start.3
  3.1 0.9 %copy-done.12 = f32[32,2048]{1,0:T(8,128)S(1)} copy-done((f32[32,2048]{1,0:T(8,128)S(1)}, f32[32,2048]{1,0:T(8,128)}, u32[]{:S(2)}) %copy-start.12) | copy-done | bytes 262168
  4.1 0.9 %copy-done.13 = f32[32,2048]{1,0:T(8,128)S(1)} copy-done((f32[32,2048]{1,0:T(8,128)S(1)}, f32[32,2048]{1,0:T(8,128)}, u32[]{:S(2)}) %copy-start.13) | copy-done | bytes 262168
  5.2 0.9 %pack.1 = (f32[488,128]{1,0:T(8,128)S(1)}, f32[488,128]{1,0:T(8,128)S(1)}, f32[488,128]{1,0:T(8,128)S(1)}, f32[488,128]{1,0:T(8,128)S(1)}) custom-call(f32[512,128]{1,0:T(8,128)S(1)} %get-tuple-element.14.re_lines, f32[512,128]{1,0:T(8,128)S(1)} %get-tuple-element.15.im_lines, f32[32,2048]{1,0:T(8,128)S(1)} %collective-permute-done.re_other, ...), custom_call_target="tpu_custom_call" | custom-call | flops 1000000 | bytes 4000000 | tf_op jit(solution)/shard_map/pack/pallas_call | solution.py:479
  6.1 0.7 %collective-permute-start.4 = (f32[488,128]{1,0:T(8,128)S(1)}, f32[488,128]{1,0:T(8,128)S(1)}, u32[]{:S(2)}, u32[]{:S(2)}) collective-permute-start(f32[488,128]{1,0:T(8,128)S(1)} %get-tuple-element.16), channel_id=1, source_target_pairs={{0,0},{1,2},{2,1},{3,3},{4,4},{5,6},{6,5},{7,7},{8,8},{9,10},{10,9... | collective-permute-start | bytes 749576 | tf_op jit(solution)/shard_map/ppermute | solution.py:500
  6.8 2.7 %collective-permute-start.6 = (f32[488,128]{1,0:T(8,128)S(1)}, f32[488,128]{1,0:T(8,128)S(1)}, u32[]{:S(2)}, u32[]{:S(2)}) collective-permute-start(f32[488,128]{1,0:T(8,128)S(1)} %get-tuple-element.17), channel_id=1, source_target_pairs={{0,4},{1,6},{2,5},{3,7},{4,0},{5,2},{6,1},{7,3},{8,12},{9,14},{10,... | collective-permute-start | bytes 749576 | tf_op jit(solution)/shard_map/ppermute | solution.py:500
  9.5 2.6 %collective-permute-start.8 = (f32[488,128]{1,0:T(8,128)S(1)}, f32[488,128]{1,0:T(8,128)S(1)}, u32[]{:S(2)}, u32[]{:S(2)}) collective-permute-start(f32[488,128]{1,0:T(8,128)S(1)} %get-tuple-element.18), channel_id=1, source_target_pairs={{0,8},{1,10},{2,9},{3,11},{4,12},{5,14},{6,13},{7,15},{8,0},{9,2},... | collective-permute-start | bytes 749576 | tf_op jit(solution)/shard_map/ppermute | solution.py:500
  12.2 3.5 %collective-permute-start.5 = (f32[488,128]{1,0:T(8,128)S(1)}, f32[488,128]{1,0:T(8,128)S(1)}, u32[]{:S(2)}, u32[]{:S(2)}) collective-permute-start(f32[488,128]{1,0:T(8,128)S(1)} %collective-permute-done.4.refs_0_), channel_id=1, source_target_pairs={{0,1},{1,0},{2,3},{3,2},{4,5},{5,4},{6,7},{7,6},{8,9},{9,8},{10,11... | collective-permute-start | bytes 749576 | tf_op jit(solution)/shard_map/ppermute | solution.py:501
  15.8 1.1 %collective-permute-done.6.refs_2_ = f32[488,128]{1,0:T(8,128)S(1)} collective-permute-done((f32[488,128]{1,0:T(8,128)S(1)}, f32[488,128]{1,0:T(8,128)S(1)}, u32[]{:S(2)}, u32[]{:S(2)}) %collective-permute-start.6) | collective-permute-done | bytes 249888 | tf_op jit(solution)/shard_map/ppermute | solution.py:500
  16.9 3.7 %collective-permute-start.7 = (f32[488,128]{1,0:T(8,128)S(1)}, f32[488,128]{1,0:T(8,128)S(1)}, u32[]{:S(2)}, u32[]{:S(2)}) collective-permute-start(f32[488,128]{1,0:T(8,128)S(1)} %collective-permute-done.6.refs_2_), channel_id=1, source_target_pairs={{0,1},{1,0},{2,3},{3,2},{4,5},{5,4},{6,7},{7,6},{8,9},{9,8},{10,11... | collective-permute-start | bytes 749576 | tf_op jit(solution)/shard_map/ppermute | solution.py:501
  20.6 12.1 %collective-permute-start.9 = (f32[488,128]{1,0:T(8,128)S(1)}, f32[488,128]{1,0:T(8,128)S(1)}, u32[]{:S(2)}, u32[]{:S(2)}) collective-permute-start(f32[488,128]{1,0:T(8,128)S(1)} %collective-permute-done.8.refs_4_), channel_id=1, source_target_pairs={{0,1},{1,0},{2,3},{3,2},{4,5},{5,4},{6,7},{7,6},{8,9},{9,8},{10,11... | collective-permute-start | bytes 749576 | tf_op jit(solution)/shard_map/ppermute | solution.py:501
  32.7 1.4 %phase.1.refs_9_ = f32[2,4,2,128,128]{4,3,2,1,0:T(8,128)S(1)} custom-call(s32[2]{0:T(128)S(1)} %copy-done.14, s32[2]{0:T(128)S(1)} %collective-permute-done.3.off_other), custom_call_target="tpu_custom_call" | custom-call | flops 10000000 | bytes 1000000 | tf_op jit(solution)/shard_map/phase/pallas_call | solution.py:503
  34.3 1.6 %spectrum.2.refs_0_ = f32[4,2,128,128]{3,2,1,0:T(8,128)S(1)} custom-call(f32[488,128]{1,0:T(8,128)S(1)} %collective-permute-done.4.refs_0_, f32[488,128]{1,0:T(8,128)S(1)} %collective-permute-done.5.refs_1_, f32[488,128]{1,0:T(8,128)S(1)} %collective-permute-done.6.refs_2_, f32[488,128]{1,0:T(8,128)S(1)} %collective-permute-done.7.refs_3_, ...), custom_call_target="tpu_custom_call" | custom-call | flops 400000000 | bytes 2000000 | tf_op jit(solution)/shard_map/spectrum/pallas_call | solution.py:514
  35.9 0.5 collective-permute-start.12
  36.6 0.9 %copy-done.5 = f32[488,128]{1,0:T(8,128)S(1)} copy-done((f32[488,128]{1,0:T(8,128)S(1)}, f32[488,128]{1,0:T(8,128)}, u32[]{:S(2)}) %copy-start.5) | copy-done | bytes 249880
  37.5 0.9 %copy-done.7 = f32[488,128]{1,0:T(8,128)S(1)} copy-done((f32[488,128]{1,0:T(8,128)S(1)}, f32[488,128]{1,0:T(8,128)}, u32[]{:S(2)}) %copy-start.7) | copy-done | bytes 249880
  38.5 0.9 %copy-done.9 = f32[488,128]{1,0:T(8,128)S(1)} copy-done((f32[488,128]{1,0:T(8,128)S(1)}, f32[488,128]{1,0:T(8,128)}, u32[]{:S(2)}) %copy-start.9) | copy-done | bytes 249880
  39.4 1.6 %spectrum.3.refs_1_ = f32[4,2,128,128]{3,2,1,0:T(8,128)S(1)} custom-call(f32[488,128]{1,0:T(8,128)S(1)} %collective-permute-done.4.refs_0_, f32[488,128]{1,0:T(8,128)S(1)} %collective-permute-done.5.refs_1_, f32[488,128]{1,0:T(8,128)S(1)} %collective-permute-done.6.refs_2_, f32[488,128]{1,0:T(8,128)S(1)} %copy-done.5, ...), custom_call_target="tpu_custom_call" | custom-call | flops 400000000 | bytes 2000000 | tf_op jit(solution)/shard_map/spectrum/pallas_call | solution.py:514
  41.1 2.2 %image.1 = (f32[4,128,128]{2,1,0:T(8,128)S(1)}, f32[4,128,128]{2,1,0:T(8,128)S(1)}) custom-call(f32[4,2,128,128]{3,2,1,0:T(8,128)S(1)} %spectrum.2.refs_0_, f32[4,2,128,128]{3,2,1,0:T(8,128)S(1)} %spectrum.3.refs_1_, f32[4,2,128,128]{3,2,1,0:T(8,128)} %collective-permute-done.12.refs_2_, f32[32,8]{1,0:T(8,128)S(1)} %copy.16.refs_3_, ...), custom_call_target="tpu_custom_call" | custom-call | flops 400000000 | bytes 2000000 | tf_op jit(solution)/shard_map/image/pallas_call | solution.py:534
  43.3 0.5 collective-permute-start.14
  43.9 1.2 %collective-permute-done.14.got = f32[4,128,128]{2,1,0:T(8,128)S(1)} collective-permute-done((f32[4,128,128]{2,1,0:T(8,128)S(1)}, f32[4,128,128]{2,1,0:T(8,128)S(1)}, u32[]{:S(2)}, u32[]{:S(2)}) %collective-permute-start.14) | collective-permute-done | bytes 262176 | tf_op jit(solution)/shard_map/ppermute | solution.py:555
  45.1 0.7 collective-permute-start.15
  45.7 6.0 %collective-permute-start.16 = (f32[256,128]{1,0:T(8,128)S(1)}, f32[256,128]{1,0:T(8,128)S(1)}, u32[]{:S(2)}, u32[]{:S(2)}) collective-permute-start(f32[256,128]{1,0:T(8,128)S(1)} %get-tuple-element.23), channel_id=1, source_target_pairs={{0,4},{1,6},{2,0},{3,2},{4,12},{5,14},{6,8},{7,10},{8,5},{9,7},{10... | collective-permute-start | bytes 393224 | tf_op jit(solution)/shard_map/ppermute | solution.py:565
  51.7 2.3 %collective-permute-start.17 = (f32[256,128]{1,0:T(8,128)S(1)}, f32[256,128]{1,0:T(8,128)S(1)}, u32[]{:S(2)}, u32[]{:S(2)}) collective-permute-start(f32[256,128]{1,0:T(8,128)S(1)} %get-tuple-element.24), channel_id=1, source_target_pairs={{0,8},{1,10},{2,12},{3,14},{4,0},{5,2},{6,4},{7,6},{8,9},{9,11},{1... | collective-permute-start | bytes 393224 | tf_op jit(solution)/shard_map/ppermute | solution.py:565
  54.0 2.7 %collective-permute-start.18 = (f32[256,128]{1,0:T(8,128)S(1)}, f32[256,128]{1,0:T(8,128)S(1)}, u32[]{:S(2)}, u32[]{:S(2)}) collective-permute-start(f32[256,128]{1,0:T(8,128)S(1)} %get-tuple-element.25), channel_id=1, source_target_pairs={{0,12},{1,14},{2,8},{3,10},{4,4},{5,6},{6,0},{7,2},{8,13},{9,15},{... | collective-permute-start | bytes 393224 | tf_op jit(solution)/shard_map/ppermute | solution.py:565
  56.7 3.8 %collective-permute-done.17.refs_2_ = f32[256,128]{1,0:T(8,128)S(1)} collective-permute-done((f32[256,128]{1,0:T(8,128)S(1)}, f32[256,128]{1,0:T(8,128)S(1)}, u32[]{:S(2)}, u32[]{:S(2)}) %collective-permute-start.17) | collective-permute-done | bytes 131104 | tf_op jit(solution)/shard_map/ppermute | solution.py:565
  60.5 6.2 %collective-permute-done.18.refs_3_ = f32[256,128]{1,0:T(8,128)S(1)} collective-permute-done((f32[256,128]{1,0:T(8,128)S(1)}, f32[256,128]{1,0:T(8,128)S(1)}, u32[]{:S(2)}, u32[]{:S(2)}) %collective-permute-start.18) | collective-permute-done | bytes 131104 | tf_op jit(solution)/shard_map/ppermute | solution.py:565
  66.7 0.9 %place.1 = (f32[32,2048]{1,0:T(8,128)}, f32[32,2048]{1,0:T(8,128)}) custom-call(f32[256,128]{1,0:T(8,128)S(1)} %collective-permute-done.15.refs_0_, f32[256,128]{1,0:T(8,128)S(1)} %collective-permute-done.16.refs_1_, f32[256,128]{1,0:T(8,128)S(1)} %collective-permute-done.17.refs_2_, f32[256,128]{1,0:T(8,128)S(1)} %collective-permute-done.18.refs_3_), custom_call_target="tpu_custom_call" | custom-call | bytes 1000000 | tf_op jit(solution)/shard_map/place/pallas_call | solution.py:566
  (50 shorter events, 0.6 us)
Async XLA Ops:
  0.6 4.6 %collective-permute-start = (f32[32,2048]{1,0:T(8,128)}, f32[32,2048]{1,0:T(8,128)S(1)}, u32[]{:S(2)}, u32[]{:S(2)}) collective-permute-start(f32[32,2048]{1,0:T(8,128)} %re_own.1), channel_id=1, source_target_pairs={{0,1},{1,0},{2,3},{3,2},{4,5},{5,4},{6,7},{7,6},{8,9},{9,8},{10,11... | collective-permute-start | bytes 786440 | tf_op jit(solution)/shard_map/ppermute | solution.py:465
  1.1 4.1 %collective-permute-start.1 = (f32[32,2048]{1,0:T(8,128)}, f32[32,2048]{1,0:T(8,128)S(1)}, u32[]{:S(2)}, u32[]{:S(2)}) collective-permute-start(f32[32,2048]{1,0:T(8,128)} %im_own.1), channel_id=1, source_target_pairs={{0,1},{1,0},{2,3},{3,2},{4,5},{5,4},{6,7},{7,6},{8,9},{9,8},{10,11... | collective-permute-start | bytes 786440 | tf_op jit(solution)/shard_map/ppermute | solution.py:465
  2.0 3.1 %collective-permute-start.2 = (f32[64,32]{1,0:T(8,128)S(1)}, f32[64,32]{1,0:T(8,128)S(1)}, u32[]{:S(2)}, u32[]{:S(2)}) collective-permute-start(f32[64,32]{1,0:T(8,128)S(1)} %bitcast.1), channel_id=1, source_target_pairs={{0,1},{1,0},{2,3},{3,2},{4,5},{5,4},{6,7},{7,6},{8,9},{9,8},{10,11... | collective-permute-start | bytes 24584 | tf_op jit(solution)/shard_map/ppermute | solution.py:465
  2.7 2.5 %collective-permute-start.3 = (s32[2]{0:T(128)S(1)}, s32[2]{0:T(128)S(1)}, u32[]{:S(2)}, u32[]{:S(2)}) collective-permute-start(s32[2]{0:T(128)S(1)} %copy-done.14), channel_id=1, source_target_pairs={{0,1},{1,0},{2,3},{3,2},{4,5},{5,4},{6,7},{7,6},{8,9},{9,8},{10,11... | collective-permute-start | bytes 32 | tf_op jit(solution)/shard_map/ppermute | solution.py:464
  3.1 0.9 %copy-start.12 = (f32[32,2048]{1,0:T(8,128)S(1)}, f32[32,2048]{1,0:T(8,128)}, u32[]{:S(2)}) copy-start(f32[32,2048]{1,0:T(8,128)} %re_own.1) | copy-start | bytes 786436
  4.1 0.9 %copy-start.13 = (f32[32,2048]{1,0:T(8,128)S(1)}, f32[32,2048]{1,0:T(8,128)}, u32[]{:S(2)}) copy-start(f32[32,2048]{1,0:T(8,128)} %im_own.1) | copy-start | bytes 786436
  6.1 6.1 %collective-permute-start.4 = (f32[488,128]{1,0:T(8,128)S(1)}, f32[488,128]{1,0:T(8,128)S(1)}, u32[]{:S(2)}, u32[]{:S(2)}) collective-permute-start(f32[488,128]{1,0:T(8,128)S(1)} %get-tuple-element.16), channel_id=1, source_target_pairs={{0,0},{1,2},{2,1},{3,3},{4,4},{5,6},{6,5},{7,7},{8,8},{9,10},{10,9... | collective-permute-start | bytes 749576 | tf_op jit(solution)/shard_map/ppermute | solution.py:500
  6.8 10.1 %collective-permute-start.6 = (f32[488,128]{1,0:T(8,128)S(1)}, f32[488,128]{1,0:T(8,128)S(1)}, u32[]{:S(2)}, u32[]{:S(2)}) collective-permute-start(f32[488,128]{1,0:T(8,128)S(1)} %get-tuple-element.17), channel_id=1, source_target_pairs={{0,4},{1,6},{2,5},{3,7},{4,0},{5,2},{6,1},{7,3},{8,12},{9,14},{10,... | collective-permute-start | bytes 749576 | tf_op jit(solution)/shard_map/ppermute | solution.py:500
  9.5 11.0 %collective-permute-start.8 = (f32[488,128]{1,0:T(8,128)S(1)}, f32[488,128]{1,0:T(8,128)S(1)}, u32[]{:S(2)}, u32[]{:S(2)}) collective-permute-start(f32[488,128]{1,0:T(8,128)S(1)} %get-tuple-element.18), channel_id=1, source_target_pairs={{0,8},{1,10},{2,9},{3,11},{4,12},{5,14},{6,13},{7,15},{8,0},{9,2},... | collective-permute-start | bytes 749576 | tf_op jit(solution)/shard_map/ppermute | solution.py:500
  12.1 22.1 %copy-start = (bf16[256,256]{1,0:T(8,128)(2,1)S(1)}, bf16[256,256]{1,0:T(8,128)(2,1)}, u32[]{:S(2)}) copy-start(bf16[256,256]{1,0:T(8,128)(2,1)} %constant.12.clone.refs_10_.refs_5_) | copy-start | bytes 393220
  12.1 22.1 %copy-start.1 = (bf16[256,256]{1,0:T(8,128)(2,1)S(1)}, bf16[256,256]{1,0:T(8,128)(2,1)}, u32[]{:S(2)}) copy-start(bf16[256,256]{1,0:T(8,128)(2,1)} %constant.13.clone.refs_11_.refs_6_) | copy-start | bytes 393220
  12.1 22.1 %copy-start.2 = (bf16[256,256]{1,0:T(8,128)(2,1)S(1)}, bf16[256,256]{1,0:T(8,128)(2,1)}, u32[]{:S(2)}) copy-start(bf16[256,256]{1,0:T(8,128)(2,1)} %constant.14.clone.refs_12_.refs_7_) | copy-start | bytes 393220
  12.1 22.1 %copy-start.3 = (bf16[256,256]{1,0:T(8,128)(2,1)S(1)}, bf16[256,256]{1,0:T(8,128)(2,1)}, u32[]{:S(2)}) copy-start(bf16[256,256]{1,0:T(8,128)(2,1)} %constant.15.clone.refs_13_.refs_8_) | copy-start | bytes 393220
  12.1 22.1 %copy-start.10 = (f32[128,128]{1,0:T(8,128)S(1)}, f32[128,128]{1,0:T(8,128)}, u32[]{:S(2)}) copy-start(f32[128,128]{1,0:T(8,128)} %constant.16.clone.refs_14_.refs_9_) | copy-start | bytes 196612
  12.1 22.1 %copy-start.11 = (f32[128,128]{1,0:T(8,128)S(1)}, f32[128,128]{1,0:T(8,128)}, u32[]{:S(2)}) copy-start(f32[128,128]{1,0:T(8,128)} %constant.17.clone.refs_15_.refs_10_) | copy-start | bytes 196612
  12.1 22.1 %copy-start.15 = (s32[2]{0:T(128)S(1)}, s32[2]{0:T(128)}, u32[]{:S(2)}) copy-start(s32[2]{0:T(128)} %refs_8_.4) | copy-start | bytes 28
  12.1 20.5 %collective-permute-start.10 = (f32[488,128]{1,0:T(8,128)S(1)}, f32[488,128]{1,0:T(8,128)S(1)}, u32[]{:S(2)}, u32[]{:S(2)}) collective-permute-start(f32[488,128]{1,0:T(8,128)S(1)} %get-tuple-element.19), channel_id=1, source_target_pairs={{0,12},{1,14},{2,13},{3,15},{4,8},{5,10},{6,9},{7,11},{8,4},{9,6},... | collective-permute-start | bytes 749576 | tf_op jit(solution)/shard_map/ppermute | solution.py:500
  12.2 21.9 %collective-permute-start.5 = (f32[488,128]{1,0:T(8,128)S(1)}, f32[488,128]{1,0:T(8,128)S(1)}, u32[]{:S(2)}, u32[]{:S(2)}) collective-permute-start(f32[488,128]{1,0:T(8,128)S(1)} %collective-permute-done.4.refs_0_), channel_id=1, source_target_pairs={{0,1},{1,0},{2,3},{3,2},{4,5},{5,4},{6,7},{7,6},{8,9},{9,8},{10,11... | collective-permute-start | bytes 749576 | tf_op jit(solution)/shard_map/ppermute | solution.py:501
  16.9 17.2 %collective-permute-start.7 = (f32[488,128]{1,0:T(8,128)S(1)}, f32[488,128]{1,0:T(8,128)S(1)}, u32[]{:S(2)}, u32[]{:S(2)}) collective-permute-start(f32[488,128]{1,0:T(8,128)S(1)} %collective-permute-done.6.refs_2_), channel_id=1, source_target_pairs={{0,1},{1,0},{2,3},{3,2},{4,5},{5,4},{6,7},{7,6},{8,9},{9,8},{10,11... | collective-permute-start | bytes 749576 | tf_op jit(solution)/shard_map/ppermute | solution.py:501
  20.6 13.6 %collective-permute-start.9 = (f32[488,128]{1,0:T(8,128)S(1)}, f32[488,128]{1,0:T(8,128)S(1)}, u32[]{:S(2)}, u32[]{:S(2)}) collective-permute-start(f32[488,128]{1,0:T(8,128)S(1)} %collective-permute-done.8.refs_4_), channel_id=1, source_target_pairs={{0,1},{1,0},{2,3},{3,2},{4,5},{5,4},{6,7},{7,6},{8,9},{9,8},{10,11... | collective-permute-start | bytes 749576 | tf_op jit(solution)/shard_map/ppermute | solution.py:501
  32.7 1.5 %collective-permute-start.11 = (f32[488,128]{1,0:T(8,128)S(1)}, f32[488,128]{1,0:T(8,128)S(1)}, u32[]{:S(2)}, u32[]{:S(2)}) collective-permute-start(f32[488,128]{1,0:T(8,128)S(1)} %collective-permute-done.10.refs_6_), channel_id=1, source_target_pairs={{0,1},{1,0},{2,3},{3,2},{4,5},{5,4},{6,7},{7,6},{8,9},{9,8},{10,11... | collective-permute-start | bytes 749576 | tf_op jit(solution)/shard_map/ppermute | solution.py:501
  34.1 2.4 %copy-start.16 = (f32[32,8]{0,1:T(8,128)S(1)}, f32[32,8]{0,1:T(8,128)}, u32[]{:S(2)}) copy-start(f32[32,8]{0,1:T(8,128)} %param.17) | copy-start | bytes 3076
  34.1 1.8 %copy-start.4 = (f32[488,128]{1,0:T(8,128)}, f32[488,128]{1,0:T(8,128)S(1)}, u32[]{:S(2)}) copy-start(f32[488,128]{1,0:T(8,128)S(1)} %collective-permute-done.7.refs_3_) | copy-start | bytes 749572
  34.1 1.8 %copy-start.6 = (f32[488,128]{1,0:T(8,128)}, f32[488,128]{1,0:T(8,128)S(1)}, u32[]{:S(2)}) copy-start(f32[488,128]{1,0:T(8,128)S(1)} %collective-permute-done.9.refs_5_) | copy-start | bytes 749572
  34.3 1.7 %copy-start.8 = (f32[488,128]{1,0:T(8,128)}, f32[488,128]{1,0:T(8,128)S(1)}, u32[]{:S(2)}) copy-start(f32[488,128]{1,0:T(8,128)S(1)} %collective-permute-done.11.refs_7_) | copy-start | bytes 749572
  35.9 5.1 %collective-permute-start.12 = (f32[4,2,128,128]{3,2,1,0:T(8,128)S(1)}, f32[4,2,128,128]{3,2,1,0:T(8,128)}, u32[]{:S(2)}, u32[]{:S(2)}) collective-permute-start(f32[4,2,128,128]{3,2,1,0:T(8,128)S(1)} %spectrum.2.refs_0_), channel_id=1, source_target_pairs={{0,1},{1,0},{2,3},{3,2},{4,5},{5,4},{6,7},{7,6},{8,9},{9,8},{10,11... | collective-permute-start | bytes 1572872 | tf_op jit(solution)/shard_map/ppermute | solution.py:530
  36.5 4.5 %collective-permute-start.13 = (f32[32,8]{1,0:T(8,128)S(1)}, f32[32,8]{1,0:T(8,128)S(1)}, u32[]{:S(2)}, u32[]{:S(2)}) collective-permute-start(f32[32,8]{1,0:T(8,128)S(1)} %copy.16.refs_3_), channel_id=1, source_target_pairs={{0,1},{1,0},{2,3},{3,2},{4,5},{5,4},{6,7},{7,6},{8,9},{9,8},{10,11... | collective-permute-start | bytes 3080 | tf_op jit(solution)/shard_map/ppermute | solution.py:465
  43.3 1.7 %collective-permute-start.14 = (f32[4,128,128]{2,1,0:T(8,128)S(1)}, f32[4,128,128]{2,1,0:T(8,128)S(1)}, u32[]{:S(2)}, u32[]{:S(2)}) collective-permute-start(f32[4,128,128]{2,1,0:T(8,128)S(1)} %get-tuple-element.21), channel_id=1, source_target_pairs={{0,1},{1,0},{2,3},{3,2},{4,5},{5,4},{6,7},{7,6},{8,9},{9,8},{10,11... | collective-permute-start | bytes 786440 | tf_op jit(solution)/shard_map/ppermute | solution.py:555
  45.1 11.6 %collective-permute-start.15 = (f32[256,128]{1,0:T(8,128)S(1)}, f32[256,128]{1,0:T(8,128)S(1)}, u32[]{:S(2)}, u32[]{:S(2)}) collective-permute-start(f32[256,128]{1,0:T(8,128)S(1)} %get-tuple-element.22), channel_id=1, source_target_pairs={{0,0},{1,2},{2,4},{3,6},{4,8},{5,10},{6,12},{7,14},{8,1},{9,3},{10... | collective-permute-start | bytes 393224 | tf_op jit(solution)/shard_map/ppermute | solution.py:565
  45.7 11.0 %collective-permute-start.16 = (f32[256,128]{1,0:T(8,128)S(1)}, f32[256,128]{1,0:T(8,128)S(1)}, u32[]{:S(2)}, u32[]{:S(2)}) collective-permute-start(f32[256,128]{1,0:T(8,128)S(1)} %get-tuple-element.23), channel_id=1, source_target_pairs={{0,4},{1,6},{2,0},{3,2},{4,12},{5,14},{6,8},{7,10},{8,5},{9,7},{10... | collective-permute-start | bytes 393224 | tf_op jit(solution)/shard_map/ppermute | solution.py:565
  51.7 8.8 %collective-permute-start.17 = (f32[256,128]{1,0:T(8,128)S(1)}, f32[256,128]{1,0:T(8,128)S(1)}, u32[]{:S(2)}, u32[]{:S(2)}) collective-permute-start(f32[256,128]{1,0:T(8,128)S(1)} %get-tuple-element.24), channel_id=1, source_target_pairs={{0,8},{1,10},{2,12},{3,14},{4,0},{5,2},{6,4},{7,6},{8,9},{9,11},{1... | collective-permute-start | bytes 393224 | tf_op jit(solution)/shard_map/ppermute | solution.py:565
  54.0 12.7 %collective-permute-start.18 = (f32[256,128]{1,0:T(8,128)S(1)}, f32[256,128]{1,0:T(8,128)S(1)}, u32[]{:S(2)}, u32[]{:S(2)}) collective-permute-start(f32[256,128]{1,0:T(8,128)S(1)} %get-tuple-element.25), channel_id=1, source_target_pairs={{0,12},{1,14},{2,8},{3,10},{4,4},{5,6},{6,0},{7,2},{8,13},{9,15},{... | collective-permute-start | bytes 393224 | tf_op jit(solution)/shard_map/ppermute | solution.py:565
  (4 other events, 3.5 us)
